TPU v7x, 1024 devices: a whole 4x8x16 slice. The times are simulated.
1024 devices in a mesh: replica: 128 (over x, y_lo, z), fsdp: 8 (over y_hi, core).
Axes of the slice: x: 4, y: 8 (y_hi: 4, y_lo: 2; y = y_hi * 2 + y_lo), z: 16, core: 2. Of those that a mesh axis runs over, the one named last changes fastest.
Arguments:
- activations: bfloat16 [128, 1152, 5120], P('replica', 'fsdp'), may hold values from -6 to 6
- cotangent: bfloat16 [128, 1152, 512], P('replica', 'fsdp'), may hold values from -0.17675781 to 0.17675781
- momentum: float32 [128, 5120, 512], P('replica', 'fsdp'), may hold values from -6 to 6
Outputs:
- momentum_next: bfloat16 [128, 5120, 512], P('replica', 'fsdp')
- update: float32 [5120, 512], P('fsdp')
All inputs are finite; a program needn't handle non-finite values.
Results may differ from a plain program's by a relative error of at most 0.015.
Values may be sent and summed in bfloat16 or wider, within the bound.
A program may use at most 32 MiB of HBM per device.

v0:
```python
import jax
import jax.numpy as jnp
from jax import lax
from jax.sharding import PartitionSpec as P

SPAN = 64
BAND = 8


momentum_decay = 0.9
norm_eps = 1e-06


def dct_basis(band_side, span_side):
    freq = jnp.arange(band_side).astype(jnp.float32)[:, None]
    place = jnp.arange(span_side).astype(jnp.float32)[None, :]
    factor = jnp.where(freq == 0.0, jnp.sqrt(1.0 / span_side), jnp.sqrt(2.0 / span_side)).astype(
        jnp.float32
    )
    return factor * jnp.cos(jnp.pi * (2.0 * place + 1.0) * freq / (2.0 * span_side))


def band_of(matrix, basis, span_side):
    blocks = matrix.reshape(
        matrix.shape[0] // span_side, span_side, matrix.shape[1] // span_side, span_side
    )
    return jnp.einsum("kp,ipjq,lq->ijkl", basis, blocks, basis, precision=lax.Precision.HIGHEST)


def expand_band(coeffs, basis, span_side):
    blocks = jnp.einsum("kp,ijkl,lq->ipjq", basis, coeffs, basis, precision=lax.Precision.HIGHEST)
    return blocks.reshape(coeffs.shape[0] * span_side, coeffs.shape[1] * span_side)


def local(activations, cotangent, momentum):
    act_rows = activations[0]
    cot_rows = cotangent[0]
    shard_rows = momentum.shape[1]
    gradient = lax.psum_scatter(
        lax.dot_general(
            act_rows, cot_rows, (((0,), (0,)), ((), ())), preferred_element_type=jnp.float32
        ).astype(jnp.bfloat16),
        "fsdp",
        scatter_dimension=0,
        tiled=True,
    ).astype(jnp.float32)
    current = momentum_decay * momentum[0] + gradient
    dct_table = dct_basis(BAND, SPAN)
    own_band = band_of(current, dct_table, SPAN)
    remaining = (current - expand_band(own_band, dct_table, SPAN)).astype(jnp.bfloat16)[None]
    flat_band = own_band.reshape(-1)
    band_total = lax.psum(flat_band, "replica")
    band_mean = band_total.reshape(own_band.shape) / lax.axis_size("replica")
    decoded = expand_band(band_mean, dct_table, SPAN)
    blocks = decoded.reshape(shard_rows // SPAN, SPAN, decoded.shape[1] // SPAN, SPAN)
    scale_rms = jnp.sqrt(jnp.mean(blocks * blocks, axis=(1, 3), keepdims=True) + norm_eps)
    update = (blocks / scale_rms).reshape(shard_rows, decoded.shape[1])
    return (remaining, update)


def solution(mesh):
    in_specs = (P("replica", "fsdp", None), P("replica", "fsdp", None), P("replica", "fsdp", None))
    out_specs = (P("replica", "fsdp", None), P("fsdp", None))
    return jax.shard_map(local, mesh=mesh, in_specs=in_specs, out_specs=out_specs, check_vma=False)
```

profile of v0, /device:TPU:48, one launch (start us, length us, event | category | flops | bytes accessed | tf_op | source)
XLA Modules:
  0.0 753.7 jit_solution(10262519883488573244)
XLA Ops:
  7.2 0.0 copy-start
  7.2 0.0 reduce-scatter.2.cloned.1.call-start
  7.2 1.3 copy-done
  8.5 4.8 convolution_convert_fusion
  13.3 0.0 reduce-scatter.2.cloned.1.call-update
  13.4 84.1 %reduce-scatter.2.cloned.1.call-done = bf16[640,512]{1,0:T(8,128)(2,1)} async-done(((bf16[5120,512]{1,0:T(8,128)(2,1)}), bf16[640,512]{1,0:T(8,128)(2,1)}) %reduce-scatter.2.cloned.1.call-update) | async-done | bytes 655376 | tf_op jit(solution)/shard_map/reduce_scatter | solution.py:39
  97.5 1.7 bitcast_add_fusion
  99.3 2.0 reshape.49
  101.3 3.4 fusion
  104.7 3.8 fusion.4
  108.5 0.6 copy.7
  109.1 0.2 reshape.51
  109.3 0.7 fusion.12
  110.0 610.9 %psum.7 = f32[5120]{0:T(1024)S(1)} all-reduce(f32[5120]{0:T(1024)S(1)} %reshape.51), channel_id=1, replica_groups=mesh['replica'=128,'fsdp'=8] {'replica'}, use_global_device_ids=true, to_apply=%region_1.2 | all-reduce | flops 5120 | bytes 40960 | tf_op jit(solution)/shard_map/psum | solution.py:52
  720.9 0.9 div.45
  721.8 1.7 fusion.9
  723.5 4.3 convolution_bitcast_fusion
  727.8 3.1 copy.6
  730.9 2.9 reshape.50
  733.8 2.4 fusion.3
  736.2 4.4 multiply_reduce_fusion
  740.6 0.3 divide_bitcast_fusion
  740.9 3.1 copy.8
  744.0 2.9 reshape.52
  (5 shorter events, 0.0 us)
Async XLA Ops:
  7.2 1.4 copy-start
  7.2 90.4 %reduce-scatter.2.cloned.1.call-start = ((), (), s32[]{:S(2)}) async-start(), calls=%async_computation.1 | async-start | bytes 5898240 | tf_op jit(solution)/shard_map/reduce_scatter | solution.py:39
Sparse Core Ops, SparseCore 0:
  13.5 83.9 reduce-scatter.1
where the time goes:
time: 754 us
  blocking collectives  611 us (81%)
  waiting for transfers between devices  84.1 us (11%)
  matrix products  23.1 us (3%)
  local copies, waits for them, and re-layouts  17 us (2%)
  between operations  14.1 us (2%)
    psum x1, blocking collectives, local(): band_total = lax.psum(flat_band, 'replica')  611 us
    reduce_scatter x1, waiting for transfers between devices, local(): lax.psum_scatter(lax.dot_general(act_rows, cot_rows, (((0,), (0,)), ((),...  84.1 us
  transfers between devices with their start and end apart: 1, of which 1 were waited for; matrix products, arithmetic and copies ran while one was open for 0% of the time, Pallas kernels for 0%

commit v1 on v0

v1 whole, which is shorter than its diff:
```python
import functools

import jax
import jax.numpy as jnp
import numpy as np
from jax import lax
from jax.experimental import pallas as pl
from jax.experimental.pallas import tpu as pltpu
from jax.sharding import PartitionSpec as P

MESH = pl.DeviceIdType.MESH
SPAN = 64
BAND = 8
DECAY = 0.9
EPS = 1e-06

T = 144
ROWS = 640
COLS = 512
NX, NYL, NZ, NH = 4, 2, 16, 4
N_REPLICA = NX * NYL * NZ
CHUNK = 128
NCHUNK = ROWS // CHUNK
TILES = 5
OWNER_STEP = 3
HIGH = lax.Precision.HIGHEST


def basis_table():
    freq = np.arange(BAND)[:, None]
    place = np.arange(SPAN)[None, :]
    scale = np.where(freq == 0, np.sqrt(1.0 / SPAN), np.sqrt(2.0 / SPAN))
    basis = scale * np.cos(np.pi * (2.0 * place + 1.0) * freq / (2.0 * SPAN))
    table = np.zeros((ROWS, 128), np.float64)
    for i in range(ROWS // SPAN):
        table[i * SPAN : (i + 1) * SPAN, i * BAND : (i + 1) * BAND] = basis.T
    return table.astype(np.float32)


def two_terms(table):
    high = table.astype(jnp.bfloat16)
    low = (table - high.astype(np.float32)).astype(jnp.bfloat16)
    return np.concatenate([high, low], axis=1)


def dot(a, b, ca, cb, precision=None):
    return lax.dot_general(
        a, b, (((ca,), (cb,)), ((), ())), preferred_element_type=jnp.float32, precision=precision
    )


def kernel(
    act, cot, mom, table, table2,
    out_next, out_update,
    act_v, buf_s, buf_g, cots, mom_v, tab, tab2, project, s_out, s_in, acc, next_v,
    vec, xbuf, corebuf, zbuf, ybuf, fin, update_v,
    load_sem, sem_s, sem_g, sem_c, send_sem, fwd_sem, s_send, s_recv, out_sem,
    x_send, x_recv, core_sem, z_send, z_recv, y_send, y_recv, f_send, f_recv, g_send, g_recv,
):
    rep = lax.axis_index("replica")
    f = lax.axis_index("fsdp")
    x = rep // (NYL * NZ)
    yl = lax.rem(rep // NZ, NYL)
    z = lax.rem(rep, NZ)
    h = f // 2
    c = lax.rem(f, 2)
    oc = 1 - c
    s = 1 - 2 * c

    def ring(v):
        return lax.rem(v + NH, NH)

    def dev(hh, cc, xx=None, yy=None, zz=None):
        xx = x if xx is None else xx
        yy = yl if yy is None else yy
        zz = z if zz is None else zz
        return {"replica": (xx * NYL + yy) * NZ + zz, "fsdp": hh * 2 + cc}

    def remote(src, dst, ss, rs, to):
        return pltpu.make_async_remote_copy(src, dst, ss, rs, device_id=to, device_id_type=MESH)

    def block(hh, cc):
        start = pl.multiple_of((hh * 2 + cc) * ROWS, ROWS)
        return act.at[0, :, pl.ds(start, ROWS)]

    loads = [
        pltpu.make_async_copy(act.at[0], act_v, load_sem.at[0]),
        pltpu.make_async_copy(cot.at[0], cots.at[2 + c], load_sem.at[1]),
        pltpu.make_async_copy(table2, tab2, load_sem.at[2]),
        pltpu.make_async_copy(table, tab, load_sem.at[3]),
        pltpu.make_async_copy(mom.at[0], mom_v, load_sem.at[4]),
        pltpu.make_async_copy(block(ring(h + s), c), buf_s.at[2 + c], load_sem.at[5]),
        pltpu.make_async_copy(block(h, c), buf_g.at[c], load_sem.at[6]),
    ]
    for copy in loads:
        copy.start()

    barrier = pltpu.get_barrier_semaphore()
    peers = [dev(h, c, xx=lax.rem(x + k, NX)) for k in range(1, NX)]
    peers += [dev(ring(h + k), c, yy=yy) for k in range(1, NH) for yy in range(NYL)]
    peers += [dev(h, c, yy=1 - yl)]
    peers += [dev(h, oc), dev(ring(h + 1), oc), dev(ring(h - 1), oc)]
    for peer in peers:
        pl.semaphore_signal(barrier, inc=1, device_id=peer, device_id_type=MESH)

    def greet(k, carry):
        pl.semaphore_signal(barrier, inc=1, device_id=dev(h, c, zz=lax.rem(z + k, NZ)), device_id_type=MESH)
        return carry

    lax.fori_loop(1, NZ, greet, 0)
    pl.semaphore_wait(barrier, len(peers) + NZ - 1)

    first = [
        remote(cot.at[0], cots.at[c], send_sem.at[0], sem_c.at[c], dev(ring(h + s), c)),
        remote(cot.at[0], cots.at[4 + c], send_sem.at[1], sem_c.at[4 + c], dev(ring(h - s), c)),
        remote(cot.at[0], cots.at[2 + c], send_sem.at[2], sem_c.at[2 + c], dev(h, oc)),
        remote(block(ring(h + s * -1), oc), buf_s.at[2 + c], send_sem.at[3], sem_s.at[2 + c], dev(h, oc)),
        remote(block(ring(h + 2), 0), buf_s.at[c], send_sem.at[4], sem_s.at[c], dev(ring(h + 1), 0)),
        remote(block(ring(h + 2), 1), buf_s.at[c], send_sem.at[5], sem_s.at[c], dev(ring(h - 1), 1)),
    ]
    second = [
        remote(block(h, oc), buf_g.at[c], send_sem.at[6], sem_g.at[c], dev(h, oc)),
        remote(block(ring(h - 1), 0), buf_g.at[2 + c], send_sem.at[7], sem_g.at[2 + c], dev(ring(h - 1), 0)),
        remote(block(ring(h + 1), 1), buf_g.at[2 + c], send_sem.at[8], sem_g.at[2 + c], dev(ring(h + 1), 1)),
    ]
    for copy in first:
        copy.start()

    for copy in loads[:3]:
        copy.wait()
    q = dot(cots[2 + c], tab2[0:COLS], 1, 0)
    q = q[:, :128] + q[:, 128:]

    def pack(band):
        return band[0:40] + pltpu.roll(band[40:80], 64, 1)

    def bands(d, carry):
        a = act_v[:, pl.ds(pl.multiple_of(d * ROWS, ROWS), ROWS)]
        p = dot(a, tab2[...], 1, 0)
        p = p[:, :128] + p[:, 128:]
        vec[d] = pack(dot(p, q, 0, 0, HIGH))
        return carry

    lax.fori_loop(0, 2 * NH, bands, 0)
    for copy in loads[3:5]:
        copy.wait()
    columns = tab[0:COLS]
    side = dot(DECAY * mom_v[...], columns, 1, 0, HIGH)
    vec[f] += pack(dot(tab[...], side, 0, 0, HIGH))

    x_copies = []
    for k in range(1, NX):
        to = lax.rem(x + k, NX)
        x_copies.append(
            remote(vec.at[pl.ds(2 * to, 2)], xbuf.at[k - 1], x_send.at[k - 1], x_recv.at[k - 1], dev(h, c, xx=to))
        )
    for copy in x_copies:
        copy.start()

    rows = tab[0:CHUNK]
    project[...] = dot(rows, rows, 1, 1, HIGH)

    def without_band(value):
        side = dot(value, tab[0:COLS], 1, 0, HIGH)
        side = dot(project[...], side, 1, 0, HIGH)
        return value - dot(side, tab[0:COLS], 1, 1, HIGH)

    forwards = [
        remote(cots.at[c], cots.at[4 + c], fwd_sem.at[0], sem_c.at[4 + c], dev(h, oc)),
        remote(cots.at[4 + c], cots.at[c], fwd_sem.at[1], sem_c.at[c], dev(h, oc)),
    ]
    first[0].wait_recv()
    forwards[0].start()
    first[1].wait_recv()
    forwards[1].start()
    first[0].wait_send()
    first[1].wait_send()
    for copy in second:
        copy.start()

    for copy in x_copies:
        copy.wait()
    vec[pl.ds(2 * x, 2)] = vec[pl.ds(2 * x, 2)] + (xbuf[0] + xbuf[1] + xbuf[2])

    core_copy = remote(vec.at[2 * x + oc], corebuf, core_sem.at[0], core_sem.at[1], dev(h, oc))
    core_copy.start()
    core_copy.wait()
    vec[2 * x + c] = vec[2 * x + c] + corebuf[...]

    mine = vec.at[2 * x + c]
    for t in range(TILES):
        owner = OWNER_STEP * t
        copy = remote(mine.at[pl.ds(8 * t, 8)], zbuf.at[z], z_send.at[t], z_recv, dev(h, c, zz=owner))

        @pl.when(z == owner)
        def _():
            zbuf[owner] = mine[pl.ds(8 * t, 8)]

        @pl.when(z != owner)
        def _():
            copy.start()

    loads[5].wait()
    remote(block(h, oc), buf_s.at[2 + oc], send_sem.at[3], sem_s.at[2 + oc], dev(h, oc)).wait_recv()
    for slot in range(2):
        remote(block(h, 0), buf_s.at[slot], send_sem.at[4], sem_s.at[slot], dev(h, oc)).wait_recv()
    remote(cot.at[0], cots.at[2 + oc], send_sem.at[2], sem_c.at[2 + oc], dev(h, oc)).wait_recv()
    remote(cot.at[0], cots.at[oc], send_sem.at[2], sem_c.at[oc], dev(h, oc)).wait_recv()
    remote(cot.at[0], cots.at[4 + oc], send_sem.at[2], sem_c.at[4 + oc], dev(h, oc)).wait_recv()

    def s_copy(k):
        at = pl.ds(pl.multiple_of(k * CHUNK, CHUNK), CHUNK)
        return remote(s_out.at[at], s_in.at[at], s_send.at[k], s_recv.at[k], dev(ring(h + s), c))

    def passed(k, carry):
        at = pl.ds(pl.multiple_of(k * CHUNK, CHUNK), CHUNK)
        a = buf_s[:, :, at].reshape(4 * T, CHUNK)
        g = dot(a, cots[0:4].reshape(4 * T, COLS), 0, 0)
        s_out[at] = without_band(g).astype(jnp.bfloat16)
        s_copy(k).start()
        return carry

    lax.fori_loop(0, NCHUNK, passed, 0)

    is_owner = jnp.logical_and(lax.rem(z, OWNER_STEP) == 0, z < OWNER_STEP * TILES)
    tile = z // OWNER_STEP

    for t in range(TILES):
        owner = OWNER_STEP * t

        @pl.when(z != owner)
        def _():
            remote(mine.at[pl.ds(8 * t, 8)], zbuf.at[z], z_send.at[t], z_recv, dev(h, c, zz=owner)).wait_send()

    def column_copy(yy):
        return remote(zbuf.at[NZ], ybuf.at[h * NYL + yl], y_send.at[yy], y_recv, dev(x, c, yy=yy))

    @pl.when(is_owner)
    def _():
        pltpu.make_async_copy(zbuf.at[pl.ds(0, NZ - 1)], zbuf.at[pl.ds(0, NZ - 1)], z_recv).wait()
        total = zbuf[0]
        for k in range(1, NZ):
            total = total + zbuf[k]
        zbuf[NZ] = total
        for yy in range(NYL):
            here = jnp.logical_and(h == x, yl == yy)

            @pl.when(here)
            def _():
                ybuf[h * NYL + yl] = total

            @pl.when(jnp.logical_not(here))
            def _():
                column_copy(yy).start()

        for yy in range(NYL):
            here = jnp.logical_and(h == x, yl == yy)

            @pl.when(jnp.logical_not(here))
            def _():
                column_copy(yy).wait_send()

    def spread(k):
        return remote(fin.at[tile], fin.at[tile], f_send.at[k], f_recv.at[tile], dev(h, c, zz=lax.rem(z + k, NZ)))

    @pl.when(jnp.logical_and(is_owner, h == x))
    def _():
        pltpu.make_async_copy(ybuf.at[pl.ds(0, 7)], ybuf.at[pl.ds(0, 7)], y_recv).wait()
        total = ybuf[0]
        for k in range(1, NH * NYL):
            total = total + ybuf[k]
        fin[tile] = total

        def go(k, carry):
            spread(k).start()
            return carry

        lax.fori_loop(1, NZ, go, 0)

        def end(k, carry):
            spread(k).wait_send()
            return carry

        lax.fori_loop(1, NZ, end, 0)

    def across(k):
        return remote(fin, fin, g_send.at[k - 1], g_recv, dev(h, c, xx=lax.rem(x + k, NX)))

    @pl.when(h == x)
    def _():
        for t in range(TILES):

            @pl.when(z != OWNER_STEP * t)
            def _():
                pltpu.make_async_copy(fin.at[t], fin.at[t], f_recv.at[t]).wait()

        for k in range(1, NX):
            across(k).start()
        for k in range(1, NX):
            across(k).wait_send()

    loads[6].wait()
    remote(block(h, oc), buf_g.at[oc], send_sem.at[6], sem_g.at[oc], dev(h, oc)).wait_recv()
    for slot in range(2, 4):
        remote(block(h, 0), buf_g.at[slot], send_sem.at[6], sem_g.at[slot], dev(h, oc)).wait_recv()

    def direct(k, carry):
        at = pl.ds(pl.multiple_of(k * CHUNK, CHUNK), CHUNK)
        a = buf_g[:, :, at].reshape(4 * T, CHUNK)
        g = dot(a, cots[2:6].reshape(4 * T, COLS), 0, 0)
        acc[at] = without_band(DECAY * mom_v[at] + g)
        return carry

    lax.fori_loop(0, NCHUNK, direct, 0)

    @pl.when(h != x)
    def _():
        pltpu.make_async_copy(fin, fin, g_recv).wait()

    total = fin[...].reshape(8 * TILES, 128) * (1.0 / N_REPLICA)
    low = lax.broadcasted_iota(jnp.int32, (8 * TILES, 128), 1) < 64
    upper = jnp.where(low, total, 0.0)
    lower = jnp.where(low, pltpu.roll(total, 64, 1), 0.0)
    shared = jnp.concatenate([upper, lower, jnp.zeros((48, 128), jnp.float32)], axis=0)
    row = lax.broadcasted_iota(jnp.int32, (128, 128), 0) // BAND
    col = lax.broadcasted_iota(jnp.int32, (128, 128), 1) // BAND
    same = (row == col).astype(jnp.float32)
    power = dot(dot(same, shared * shared, 1, 0, HIGH), same, 1, 0, HIGH) * (1.0 / (SPAN * SPAN))
    shared = shared / jnp.sqrt(power + EPS)
    wide = dot(shared, tab[0:COLS], 1, 1, HIGH)
    update_v[...] = dot(tab[...], wide, 1, 0, HIGH)
    update_copy = pltpu.make_async_copy(update_v, out_update, out_sem.at[NCHUNK])
    update_copy.start()

    def out_copy(k):
        at = pl.ds(pl.multiple_of(k * CHUNK, CHUNK), CHUNK)
        return pltpu.make_async_copy(next_v.at[at], out_next.at[0, at], out_sem.at[k])

    def finish(k, carry):
        at = pl.ds(pl.multiple_of(k * CHUNK, CHUNK), CHUNK)
        s_copy(k).wait_recv()
        next_v[at] = (acc[at] + s_in[at].astype(jnp.float32)).astype(jnp.bfloat16)
        out_copy(k).start()
        return carry

    lax.fori_loop(0, NCHUNK, finish, 0)

    def drain(k, carry):
        s_copy(k).wait_send()
        out_copy(k).wait()
        return carry

    lax.fori_loop(0, NCHUNK, drain, 0)
    update_copy.wait()
    for copy in first[2:] + second + forwards:
        copy.wait_send()


def solution(mesh):
    assert mesh.shape["replica"] == N_REPLICA and mesh.shape["fsdp"] == 2 * NH
    table = basis_table()
    table2 = two_terms(table)
    f32, b16, dma = jnp.float32, jnp.bfloat16, pltpu.SemaphoreType.DMA

    def local(activations, cotangent, momentum):
        return pl.pallas_call(
            kernel,
            out_shape=(
                jax.ShapeDtypeStruct((1, ROWS, COLS), b16),
                jax.ShapeDtypeStruct((ROWS, COLS), f32),
            ),
            in_specs=[pl.BlockSpec(memory_space=pl.ANY)] * 5,
            out_specs=(pl.BlockSpec(memory_space=pl.ANY),) * 2,
            scratch_shapes=[
                pltpu.VMEM((T, 2 * NH * ROWS), b16),
                pltpu.VMEM((4, T, ROWS), b16),
                pltpu.VMEM((4, T, ROWS), b16),
                pltpu.VMEM((6, T, COLS), b16),
                pltpu.VMEM((ROWS, COLS), f32),
                pltpu.VMEM((ROWS, 128), f32),
                pltpu.VMEM((ROWS, 256), b16),
                pltpu.VMEM((CHUNK, CHUNK), f32),
                pltpu.VMEM((ROWS, COLS), b16),
                pltpu.VMEM((ROWS, COLS), b16),
                pltpu.VMEM((ROWS, COLS), f32),
                pltpu.VMEM((ROWS, COLS), b16),
                pltpu.VMEM((2 * NH, 8 * TILES, 128), f32),
                pltpu.VMEM((NX - 1, 2, 8 * TILES, 128), f32),
                pltpu.VMEM((8 * TILES, 128), f32),
                pltpu.VMEM((NZ + 1, 8, 128), f32),
                pltpu.VMEM((NH * NYL, 8, 128), f32),
                pltpu.VMEM((TILES, 8, 128), f32),
                pltpu.VMEM((ROWS, COLS), f32),
                dma((7,)), dma((4,)), dma((4,)), dma((6,)), dma((9,)), dma((2,)),
                dma((NCHUNK,)), dma((NCHUNK,)), dma((NCHUNK + 1,)),
                dma((NX - 1,)), dma((NX - 1,)), dma((2,)),
                dma((TILES,)), dma, dma((NYL,)), dma,
                dma((NZ,)), dma((TILES,)), dma((NX - 1,)), dma,
            ],
            compiler_params=pltpu.CompilerParams(
                collective_id=0, has_side_effects=True, vmem_limit_bytes=48 * 1024 * 1024
            ),
            cost_estimate=pl.CostEstimate(flops=2_000_000_000, bytes_accessed=6_000_000, transcendentals=0),
        )(activations, cotangent, momentum, jnp.asarray(table), jnp.asarray(table2))

    in_specs = (P("replica", "fsdp", None),) * 3
    out_specs = (P("replica", "fsdp", None), P("fsdp", None))
    return jax.shard_map(local, mesh=mesh, in_specs=in_specs, out_specs=out_specs, check_vma=False)
```

time: 754 us -> 88.3 us (0.12)
  the two profiles are of different devices: /device:TPU:48 before, /device:TPU:1 now
where the time goes in v1:
time: 88.3 us; the launch traced here: 87.1 us
  Pallas kernels  79 us (89%)
  local copies, waits for them, and re-layouts  7.43 us (8%)
    pallas_call x1, Pallas kernels, local(): pl.pallas_call(kernel, out_shape=(jax.ShapeDtypeStruct((1, ROWS, COLS), b...  79 us
    unnamed x12, local copies, waits for them, and re-layouts  7.43 us

profile of v1, /device:TPU:1, one launch (start us, length us, event | category | flops | bytes accessed | tf_op | source)
XLA Modules:
  0.0 87.1 jit_solution(12300317478376215201)
XLA Ops:
  0.6 0.0 copy-start
  0.6 1.4 %copy-done = bf16[1,144,5120]{2,1,0:T(8,128)(2,1)S(1)} copy-done((bf16[1,144,5120]{2,1,0:T(8,128)(2,1)S(1)}, bf16[1,144,5120]{2,1,0:T(8,128)(2,1)}, u32[]{:S(2)}) %copy-start) | copy-done | bytes 1474584
  2.0 0.0 copy-start.1
  2.0 1.3 %copy-done.1 = f32[1,640,512]{2,1,0:T(8,128)S(1)} copy-done((f32[1,640,512]{2,1,0:T(8,128)S(1)}, f32[1,640,512]{2,1,0:T(8,128)}, u32[]{:S(2)}) %copy-start.1) | copy-done | bytes 1310744
  3.3 0.0 copy-start.2
  3.3 0.9 %copy-done.2 = bf16[1,144,512]{2,1,0:T(8,128)(2,1)S(1)} copy-done((bf16[1,144,512]{2,1,0:T(8,128)(2,1)S(1)}, bf16[1,144,512]{2,1,0:T(8,128)(2,1)}, u32[]{:S(2)}) %copy-start.2) | copy-done | bytes 147480
  4.2 0.0 copy-start.3
  4.2 1.0 %copy-done.3 = bf16[640,256]{1,0:T(8,128)(2,1)S(1)} copy-done((bf16[640,256]{1,0:T(8,128)(2,1)S(1)}, bf16[640,256]{1,0:T(8,128)(2,1)}, u32[]{:S(2)}) %copy-start.3) | copy-done | bytes 327704
  5.2 0.0 copy-start.4
  5.2 1.0 %copy-done.4 = f32[640,128]{1,0:T(8,128)S(1)} copy-done((f32[640,128]{1,0:T(8,128)S(1)}, f32[640,128]{1,0:T(8,128)}, u32[]{:S(2)}) %copy-start.4) | copy-done | bytes 327704
  6.2 79.0 %shard_map.68 = (bf16[1,640,512]{2,1,0:T(8,128)(2,1)S(1)}, f32[640,512]{1,0:T(8,128)S(1)}) custom-call(bf16[1,144,5120]{2,1,0:T(8,128)(2,1)S(1)} %copy-done, bf16[1,144,512]{2,1,0:T(8,128)(2,1)S(1)} %copy-done.2, f32[1,640,512]{2,1,0:T(8,128)S(1)} %copy-done.1, f32[640,128]{1,0:T(8,128)S(1)} %copy-done.4, bf16[640,256]{1,0:T(8,128)(2,1)S(1)} %copy-done.3), custom_call_target="tpu_custom_call" | custom-call | flops 2000000000 | bytes 6000000 | tf_op jit(solution)/shard_map/pallas_call | solution.py:366
  85.2 0.8 copy.9
  86.0 1.1 %copy.10 = f32[640,512]{1,0:T(8,128)} copy(f32[640,512]{1,0:T(8,128)S(1)} %get-tuple-element.5) | data formatting | bytes 2621440
Async XLA Ops:
  0.6 1.4 %copy-start = (bf16[1,144,5120]{2,1,0:T(8,128)(2,1)S(1)}, bf16[1,144,5120]{2,1,0:T(8,128)(2,1)}, u32[]{:S(2)}) copy-start(bf16[1,144,5120]{2,1,0:T(8,128)(2,1)} %act.1) | copy-start | bytes 4423684
  2.0 1.3 %copy-start.1 = (f32[1,640,512]{2,1,0:T(8,128)S(1)}, f32[1,640,512]{2,1,0:T(8,128)}, u32[]{:S(2)}) copy-start(f32[1,640,512]{2,1,0:T(8,128)} %mom.1) | copy-start | bytes 3932164
  3.3 0.9 %copy-start.2 = (bf16[1,144,512]{2,1,0:T(8,128)(2,1)S(1)}, bf16[1,144,512]{2,1,0:T(8,128)(2,1)}, u32[]{:S(2)}) copy-start(bf16[1,144,512]{2,1,0:T(8,128)(2,1)} %cot.1) | copy-start | bytes 442372
  4.2 1.0 %copy-start.3 = (bf16[640,256]{1,0:T(8,128)(2,1)S(1)}, bf16[640,256]{1,0:T(8,128)(2,1)}, u32[]{:S(2)}) copy-start(bf16[640,256]{1,0:T(8,128)(2,1)} %constant.5.clone.table2) | copy-start | bytes 983044
  5.2 1.0 %copy-start.4 = (f32[640,128]{1,0:T(8,128)S(1)}, f32[640,128]{1,0:T(8,128)}, u32[]{:S(2)}) copy-start(f32[640,128]{1,0:T(8,128)} %constant.4.clone.table) | copy-start | bytes 983044

commit v2 on v0

v2 whole, which is shorter than its diff:
```python
import functools

import jax
import jax.numpy as jnp
import numpy as np
from jax import lax
from jax.experimental import pallas as pl
from jax.experimental.pallas import tpu as pltpu
from jax.sharding import PartitionSpec as P

MESH = pl.DeviceIdType.MESH
SPAN = 64
BAND = 8
DECAY = 0.9
EPS = 1e-06

T = 144
ROWS = 640
COLS = 512
NX, NYL, NZ, NH = 4, 2, 16, 4
N_REPLICA = NX * NYL * NZ
CHUNK = 128
NCHUNK = ROWS // CHUNK
TILES = 5
OWNER = NZ - TILES
HIGH = lax.Precision.HIGHEST


def basis_table():
    freq = np.arange(BAND)[:, None]
    place = np.arange(SPAN)[None, :]
    scale = np.where(freq == 0, np.sqrt(1.0 / SPAN), np.sqrt(2.0 / SPAN))
    basis = scale * np.cos(np.pi * (2.0 * place + 1.0) * freq / (2.0 * SPAN))
    table = np.zeros((CHUNK, 128), np.float64)
    for i in range(CHUNK // SPAN):
        table[i * SPAN : (i + 1) * SPAN, i * BAND : (i + 1) * BAND] = basis.T
    return table.astype(np.float32)


def split(value):
    high = value.astype(jnp.bfloat16)
    return high, (value - high.astype(jnp.float32)).astype(jnp.bfloat16)


def turn(value, by):
    return value if by == 0 else pltpu.roll(value, by, 1)


def dot(a, b, ca, cb, precision=None):
    return lax.dot_general(
        a, b, (((ca,), (cb,)), ((), ())), preferred_element_type=jnp.float32, precision=precision
    )


def kernel(
    act, cot, mom, table,
    out_next, out_bands,
    act_v, buf_s, buf_g, cots, mom_v, tab, tab2, project, side_v, p_v, s_out, s_in, acc, next_v,
    vec, xbuf, corebuf, zbuf, ybuf, fin,
    go_sem, far_sem, load_sem, sem_s, sem_g, sem_c, send_sem, fwd_sem, s_send, s_recv, out_sem,
    x_send, x_recv, core_sem, z_send, z_recv, y_send, y_recv, f_send, f_recv, g_send, g_recv,
):
    rep = lax.axis_index("replica")
    f = lax.axis_index("fsdp")
    x = rep // (NYL * NZ)
    yl = lax.rem(rep // NZ, NYL)
    z = lax.rem(rep, NZ)
    h = f // 2
    c = lax.rem(f, 2)
    oc = 1 - c
    s = 1 - 2 * c

    def ring(v):
        return lax.rem(v + NH, NH)

    def dev(hh, cc, xx=None, yy=None, zz=None):
        xx = x if xx is None else xx
        yy = yl if yy is None else yy
        zz = z if zz is None else zz
        return {"replica": (xx * NYL + yy) * NZ + zz, "fsdp": hh * 2 + cc}

    def remote(src, dst, ss, rs, to):
        return pltpu.make_async_remote_copy(src, dst, ss, rs, device_id=to, device_id_type=MESH)

    def block(hh, cc):
        start = pl.multiple_of((hh * 2 + cc) * ROWS, ROWS)
        return act.at[0, :, pl.ds(start, ROWS)]

    loads = [
        pltpu.make_async_copy(table, tab, load_sem.at[0]),
        pltpu.make_async_copy(cot.at[0], cots.at[2 + c], load_sem.at[1]),
        pltpu.make_async_copy(mom.at[0], mom_v, load_sem.at[2]),
        pltpu.make_async_copy(block(ring(h + s), c), buf_s.at[2 + c], load_sem.at[3]),
        pltpu.make_async_copy(block(h, c), buf_g.at[c], load_sem.at[4]),
    ]
    loads += [
        pltpu.make_async_copy(act.at[0, :, pl.ds(d * ROWS, ROWS)], act_v.at[d], load_sem.at[5 + d])
        for d in range(2 * NH)
    ]
    for copy in loads:
        copy.start()

    barrier = pltpu.get_barrier_semaphore()
    first_one = f == 0

    @pl.when(jnp.logical_not(first_one))
    def _():
        pl.semaphore_signal(barrier, inc=1, device_id={"replica": rep, "fsdp": 0}, device_id_type=MESH)

    loads[0].wait()
    rows = tab[...]
    for k in range(NCHUNK):
        high, low = split(turn(rows, 2 * BAND * k))
        tab2[k * CHUNK : (k + 1) * CHUNK] = jnp.concatenate([high, low], axis=1)
    high, low = split(dot(rows, rows, 1, 1, HIGH))
    project[...] = jnp.concatenate([high, low], axis=1)

    @pl.when(first_one)
    def _():
        pl.semaphore_wait(barrier, 2 * NH - 1)
        for k in range(1, 2 * NH):
            pl.semaphore_signal(go_sem, inc=1, device_id={"replica": rep, "fsdp": k}, device_id_type=MESH)

    @pl.when(jnp.logical_not(first_one))
    def _():
        pl.semaphore_wait(go_sem, 1)

    first = [
        remote(cot.at[0], cots.at[c], send_sem.at[0], sem_c.at[c], dev(ring(h + s), c)),
        remote(cot.at[0], cots.at[4 + c], send_sem.at[1], sem_c.at[4 + c], dev(ring(h - s), c)),
        remote(cot.at[0], cots.at[2 + c], send_sem.at[2], sem_c.at[2 + c], dev(h, oc)),
        remote(block(ring(h + s * -1), oc), buf_s.at[2 + c], send_sem.at[3], sem_s.at[2 + c], dev(h, oc)),
        remote(block(ring(h + 2), 0), buf_s.at[c], send_sem.at[4], sem_s.at[c], dev(ring(h + 1), 0)),
        remote(block(ring(h + 2), 1), buf_s.at[c], send_sem.at[5], sem_s.at[c], dev(ring(h - 1), 1)),
    ]
    second = [
        remote(block(h, oc), buf_g.at[c], send_sem.at[6], sem_g.at[c], dev(h, oc)),
        remote(block(ring(h - 1), 0), buf_g.at[2 + c], send_sem.at[7], sem_g.at[2 + c], dev(ring(h - 1), 0)),
        remote(block(ring(h + 1), 1), buf_g.at[2 + c], send_sem.at[8], sem_g.at[2 + c], dev(ring(h + 1), 1)),
    ]
    for copy in first:
        copy.start()

    far = [dev(h, c, xx=lax.rem(x + k, NX)) for k in range(1, NX)]

    @pl.when(jnp.logical_not(first_one))
    def _():
        for peer in far:
            pl.semaphore_signal(barrier, inc=1, device_id=peer, device_id_type=MESH)
        for k in range(NH):

            @pl.when(k + c > 0)
            def _():
                pl.semaphore_signal(barrier, inc=1, device_id=dev(k, c, yy=1 - yl), device_id_type=MESH)

        def greet(k, carry):
            pl.semaphore_signal(barrier, inc=1, device_id=dev(h, c, zz=lax.rem(z + k, NZ)), device_id_type=MESH)
            return carry

        lax.fori_loop(1, NZ, greet, 0)

    for copy in loads[1:3] + loads[5:]:
        copy.wait()
    columns = tab2[0:COLS]

    def sides(value):
        high, low = split(value)
        wide = dot(high, columns, 1, 0)
        return wide[:, :128] + wide[:, 128:] + dot(low, columns[:, :128], 1, 0)

    def pack(band):
        return band[0:40] + pltpu.roll(band[40:80], 64, 1)

    q = dot(cots[2 + c], columns, 1, 0)
    q = q[:, :128] + q[:, 128:]
    q_high, q_low = split(q)
    q_both = (q_high.astype(jnp.float32) + pltpu.roll(q_low.astype(jnp.float32), 64, 1)).astype(jnp.bfloat16)
    q_all = jnp.concatenate([q_both, q_high], axis=0)
    p = dot(act_v[...].reshape(2 * NH * T, ROWS), tab2[...], 1, 0)
    p = p[:, :128] + p[:, 128:]
    for d in range(2 * NH):
        p_high, p_low = split(p[d * T : (d + 1) * T])
        p_v[0:T, d * 128 : (d + 1) * 128] = p_high
        p_v[T : 2 * T, d * 128 : (d + 1) * 128] = p_low
    bands = dot(q_all, p_v[...], 0, 0)
    bands = bands[0:64] + bands[64:128]
    for d in range(2 * NH):
        part = bands[:, d * 128 : (d + 1) * 128]
        vec[d] = pack(jnp.concatenate([part, jnp.zeros_like(part)], axis=0).T)
    side_v[...] = sides(DECAY * mom_v[...])
    side_high, side_low = split(side_v[...])
    own = dot(tab2[...], side_high, 0, 0)
    own = own[0:128] + own[128:256] + dot(tab2[:, :128], side_low, 0, 0)
    vec[f] += pack(own)

    forwards = [
        remote(cots.at[c], cots.at[4 + c], fwd_sem.at[0], sem_c.at[4 + c], dev(h, oc)),
        remote(cots.at[4 + c], cots.at[c], fwd_sem.at[1], sem_c.at[c], dev(h, oc)),
    ]
    first[0].wait_recv()
    forwards[0].start()
    first[1].wait_recv()
    forwards[1].start()
    first[0].wait_send()
    first[1].wait_send()
    for copy in second:
        copy.start()

    @pl.when(jnp.logical_not(first_one))
    def _():
        pl.semaphore_wait(barrier, len(far) + NZ - 1 + NH - 1 + c)

    @pl.when(f == 1)
    def _():
        pl.semaphore_signal(far_sem, inc=1, device_id={"replica": rep, "fsdp": 0}, device_id_type=MESH)

    @pl.when(first_one)
    def _():
        pl.semaphore_wait(far_sem, 1)

    is_owner = z >= OWNER
    tile = lax.rem(z + TILES, NZ)

    mine = vec.at[2 * x + c]

    def s_copy(k):
        at = pl.ds(pl.multiple_of(k * CHUNK, CHUNK), CHUNK)
        return remote(s_out.at[at], s_in.at[at], s_send.at[k], s_recv.at[k], dev(ring(h + s), c))

    def low_part(side):
        high, low = split(side)
        rows = []
        for k in range(NCHUNK):
            top = high[k * CHUNK : (k + 1) * CHUNK]
            both = jnp.concatenate([top, top], axis=0)
            rows.append(dot(project[...], both, 1, 0) + dot(project[:, :128], low[k * CHUNK : (k + 1) * CHUNK], 1, 0))
        high, low = split(jnp.concatenate(rows, axis=0))
        return dot(jnp.concatenate([high, high], axis=1), columns, 1, 1) + dot(low, columns[:, :128], 1, 1)

    def near_sums():
        x_copies = []
        for k in range(1, NX):
            to = lax.rem(x + k, NX)
            x_copies.append(
                remote(vec.at[pl.ds(2 * to, 2)], xbuf.at[k - 1], x_send.at[k - 1], x_recv.at[k - 1], dev(h, c, xx=to))
            )
        for copy in x_copies:
            copy.start()

        for copy in x_copies:
            copy.wait()
        vec[pl.ds(2 * x, 2)] = vec[pl.ds(2 * x, 2)] + (xbuf[0] + xbuf[1] + xbuf[2])

        core_copy = remote(vec.at[2 * x + oc], corebuf, core_sem.at[0], core_sem.at[1], dev(h, oc))
        core_copy.start()
        core_copy.wait()
        vec[2 * x + c] = vec[2 * x + c] + corebuf[...]

        for t in range(TILES):
            owner = OWNER + t
            copy = remote(mine.at[pl.ds(8 * t, 8)], zbuf.at[z], z_send.at[t], z_recv, dev(h, c, zz=owner))

            @pl.when(z == owner)
            def _():
                zbuf[owner] = mine[pl.ds(8 * t, 8)]

            @pl.when(z != owner)
            def _():
                copy.start()

    def passed_on():
        loads[3].wait()
        remote(block(h, oc), buf_s.at[2 + oc], send_sem.at[3], sem_s.at[2 + oc], dev(h, oc)).wait_recv()
        for slot in range(2):
            remote(block(h, 0), buf_s.at[slot], send_sem.at[4], sem_s.at[slot], dev(h, oc)).wait_recv()
        remote(cot.at[0], cots.at[2 + oc], send_sem.at[2], sem_c.at[2 + oc], dev(h, oc)).wait_recv()
        remote(cot.at[0], cots.at[oc], send_sem.at[2], sem_c.at[oc], dev(h, oc)).wait_recv()
        remote(cot.at[0], cots.at[4 + oc], send_sem.at[2], sem_c.at[4 + oc], dev(h, oc)).wait_recv()

        acc[...] = dot(buf_s[...].reshape(4 * T, ROWS), cots[0:4].reshape(4 * T, COLS), 0, 0)
        s_out[...] = (acc[...] - low_part(sides(acc[...]))).astype(jnp.bfloat16)
        for k in range(NCHUNK):
            s_copy(k).start()

    def owner_sums():
        for t in range(TILES):
            owner = OWNER + t

            @pl.when(z != owner)
            def _():
                remote(mine.at[pl.ds(8 * t, 8)], zbuf.at[z], z_send.at[t], z_recv, dev(h, c, zz=owner)).wait_send()

        def column_copy(yy):
            return remote(zbuf.at[NZ], ybuf.at[h * NYL + yl], y_send.at[yy], y_recv, dev(x, c, yy=yy))

        @pl.when(is_owner)
        def _():
            pltpu.make_async_copy(zbuf.at[pl.ds(0, NZ - 1)], zbuf.at[pl.ds(0, NZ - 1)], z_recv).wait()
            total = zbuf[0]
            for k in range(1, NZ):
                total = total + zbuf[k]
            zbuf[NZ] = total
            for yy in range(NYL):
                here = jnp.logical_and(h == x, yl == yy)

                @pl.when(here)
                def _():
                    ybuf[h * NYL + yl] = total

                @pl.when(jnp.logical_not(here))
                def _():
                    column_copy(yy).start()

            for yy in range(NYL):
                here = jnp.logical_and(h == x, yl == yy)

                @pl.when(jnp.logical_not(here))
                def _():
                    column_copy(yy).wait_send()

        def spread(k):
            return remote(fin.at[tile], fin.at[tile], f_send.at[k], f_recv.at[tile], dev(h, c, zz=lax.rem(z + k, NZ)))

        @pl.when(jnp.logical_and(is_owner, h == x))
        def _():
            pltpu.make_async_copy(ybuf.at[pl.ds(0, 7)], ybuf.at[pl.ds(0, 7)], y_recv).wait()
            total = ybuf[0]
            for k in range(1, NH * NYL):
                total = total + ybuf[k]
            fin[tile] = total

            def go(k, carry):
                spread(k).start()
                return carry

            lax.fori_loop(1, NZ, go, 0)

            def end(k, carry):
                spread(k).wait_send()
                return carry

            lax.fori_loop(1, NZ, end, 0)

    def across_sums():
        def across(k):
            return remote(fin, fin, g_send.at[k - 1], g_recv, dev(h, c, xx=lax.rem(x + k, NX)))

        @pl.when(h == x)
        def _():
            for t in range(TILES):

                @pl.when(z != OWNER + t)
                def _():
                    pltpu.make_async_copy(fin.at[t], fin.at[t], f_recv.at[t]).wait()

            for k in range(1, NX):
                across(k).start()
            for k in range(1, NX):
                across(k).wait_send()

    def direct():
        loads[4].wait()
        remote(block(h, oc), buf_g.at[oc], send_sem.at[6], sem_g.at[oc], dev(h, oc)).wait_recv()
        for slot in range(2, 4):
            remote(block(h, 0), buf_g.at[slot], send_sem.at[6], sem_g.at[slot], dev(h, oc)).wait_recv()

        acc[...] = dot(buf_g[...].reshape(4 * T, ROWS), cots[2:6].reshape(4 * T, COLS), 0, 0)
        acc[...] = DECAY * mom_v[...] + acc[...] - low_part(side_v[...] + sides(acc[...]))

    def bands_out():
        @pl.when(h != x)
        def _():
            pltpu.make_async_copy(fin, fin, g_recv).wait()

        bands_copy = pltpu.make_async_copy(fin, out_bands, out_sem.at[NCHUNK])
        bands_copy.start()
        bands_copy.wait()

    near_sums()
    passed_on()
    owner_sums()
    direct()
    across_sums()

    def out_copy(k):
        at = pl.ds(pl.multiple_of(k * CHUNK, CHUNK), CHUNK)
        return pltpu.make_async_copy(next_v.at[at], out_next.at[0, at], out_sem.at[k])

    def finish(k, carry):
        at = pl.ds(pl.multiple_of(k * CHUNK, CHUNK), CHUNK)
        s_copy(k).wait_recv()
        next_v[at] = (acc[at] + s_in[at].astype(jnp.float32)).astype(jnp.bfloat16)
        out_copy(k).start()
        return carry

    lax.fori_loop(0, NCHUNK, finish, 0)
    bands_out()

    def drain(k, carry):
        s_copy(k).wait_send()
        out_copy(k).wait()
        return carry

    lax.fori_loop(0, NCHUNK, drain, 0)
    for copy in first[2:] + second + forwards:
        copy.wait_send()


def close(bands, table, value, out_next, out_update, update_v, value_v, sem):
    held = pltpu.make_async_copy(value, value_v, sem.at[NCHUNK])
    held.start()
    total = bands[...].reshape(8 * TILES, 128) * (1.0 / N_REPLICA)
    left = lax.broadcasted_iota(jnp.int32, (8 * TILES, 128), 1) < 64
    upper = jnp.where(left, total, 0.0)
    lower = jnp.where(left, pltpu.roll(total, 64, 1), 0.0)
    shared = jnp.concatenate([upper, lower, jnp.zeros((48, 128), jnp.float32)], axis=0)
    row = lax.broadcasted_iota(jnp.int32, (128, 128), 0) // BAND
    col = lax.broadcasted_iota(jnp.int32, (128, 128), 1) // BAND
    same = (row == col).astype(jnp.float32)
    power = dot(dot(same, shared * shared, 1, 0, HIGH), same, 1, 0, HIGH) * (1.0 / (SPAN * SPAN))
    shared = shared / jnp.sqrt(power + EPS)
    held.wait()
    copy = pltpu.make_async_copy(value_v, out_next, sem.at[NCHUNK])
    copy.start()
    rows = table[...]
    columns = [split(turn(rows, 2 * BAND * k)) for k in range(COLS // CHUNK)]
    high, low = split(shared)
    left, right = jnp.concatenate([high, high], axis=1), low
    wide = [
        dot(left, jnp.concatenate([a, b], axis=1), 1, 1) + dot(right, a, 1, 1) for a, b in columns
    ]
    high, low = split(jnp.concatenate(wide, axis=1))
    below = jnp.concatenate([high, low], axis=0)
    copies = []
    for k in range(NCHUNK):
        at = pl.ds(k * CHUNK, CHUNK)
        a, b = split(turn(rows, 2 * BAND * k))
        update_v[at] = dot(jnp.concatenate([a, a], axis=1), below, 1, 0) + dot(b, high, 1, 0)
        copies.append(pltpu.make_async_copy(update_v.at[at], out_update.at[at], sem.at[k]))
        copies[-1].start()
    for each in copies:
        each.wait()
    copy.wait()


def solution(mesh):
    assert mesh.shape["replica"] == N_REPLICA and mesh.shape["fsdp"] == 2 * NH
    table = basis_table()
    f32, b16, dma = jnp.float32, jnp.bfloat16, pltpu.SemaphoreType.DMA

    def local(activations, cotangent, momentum):
        rows = jnp.asarray(table)
        value, bands = pl.pallas_call(
            kernel,
            out_shape=(
                jax.ShapeDtypeStruct((1, ROWS, COLS), b16),
                jax.ShapeDtypeStruct((TILES, 8, 128), f32),
            ),
            in_specs=[pl.BlockSpec(memory_space=pl.ANY)] * 4,
            out_specs=(pl.BlockSpec(memory_space=pl.ANY),) * 2,
            scratch_shapes=[
                pltpu.VMEM((2 * NH, T, ROWS), b16),
                pltpu.VMEM((4, T, ROWS), b16),
                pltpu.VMEM((4, T, ROWS), b16),
                pltpu.VMEM((6, T, COLS), b16),
                pltpu.VMEM((ROWS, COLS), f32),
                pltpu.VMEM((CHUNK, 128), f32),
                pltpu.VMEM((ROWS, 256), b16),
                pltpu.VMEM((CHUNK, 256), b16),
                pltpu.VMEM((ROWS, 128), f32),
                pltpu.VMEM((2 * T, 2 * NH * 128), b16),
                pltpu.VMEM((ROWS, COLS), b16),
                pltpu.VMEM((ROWS, COLS), b16),
                pltpu.VMEM((ROWS, COLS), f32),
                pltpu.VMEM((ROWS, COLS), b16),
                pltpu.VMEM((2 * NH, 8 * TILES, 128), f32),
                pltpu.VMEM((NX - 1, 2, 8 * TILES, 128), f32),
                pltpu.VMEM((8 * TILES, 128), f32),
                pltpu.VMEM((NZ + 1, 8, 128), f32),
                pltpu.VMEM((NH * NYL, 8, 128), f32),
                pltpu.VMEM((TILES, 8, 128), f32),
                pltpu.SemaphoreType.REGULAR, pltpu.SemaphoreType.REGULAR,
                dma((5 + 2 * NH,)), dma((4,)), dma((4,)), dma((6,)), dma((9,)), dma((2,)),
                dma((NCHUNK,)), dma((NCHUNK,)), dma((NCHUNK + 1,)),
                dma((NX - 1,)), dma((NX - 1,)), dma((2,)),
                dma((TILES,)), dma, dma((NYL,)), dma,
                dma((NZ,)), dma((TILES,)), dma((NX - 1,)), dma,
            ],
            compiler_params=pltpu.CompilerParams(
                collective_id=0, has_side_effects=True, vmem_limit_bytes=60 * 1024 * 1024
            ),
            cost_estimate=pl.CostEstimate(flops=2_000_000_000, bytes_accessed=6_000_000, transcendentals=0),
        )(activations, cotangent, momentum, rows)
        return pl.pallas_call(
            close,
            out_shape=(
                jax.ShapeDtypeStruct((1, ROWS, COLS), b16),
                jax.ShapeDtypeStruct((ROWS, COLS), f32),
            ),
            in_specs=[pl.BlockSpec(memory_space=pltpu.VMEM)] * 2 + [pl.BlockSpec(memory_space=pl.ANY)],
            out_specs=(pl.BlockSpec(memory_space=pl.ANY),) * 2,
            scratch_shapes=[pltpu.VMEM((ROWS, COLS), f32), pltpu.VMEM((1, ROWS, COLS), b16), dma((NCHUNK + 1,))],
            compiler_params=pltpu.CompilerParams(vmem_limit_bytes=60 * 1024 * 1024),
            cost_estimate=pl.CostEstimate(flops=500_000_000, bytes_accessed=4_000_000, transcendentals=0),
        )(bands, rows, value)

    in_specs = (P("replica", "fsdp", None),) * 3
    out_specs = (P("replica", "fsdp", None), P("fsdp", None))
    return jax.shard_map(local, mesh=mesh, in_specs=in_specs, out_specs=out_specs, check_vma=False)
```

time: 754 us -> 77.4 us (0.10)
  the two profiles are of different devices: /device:TPU:48 before, /device:TPU:1 now
where the time goes in v2:
time: 77.4 us; the launch traced here: 76.5 us
  Pallas kernels  75.8 us (98%)
    pallas_call x1, Pallas kernels, local(): pl.pallas_call(kernel, out_shape=(jax.ShapeDtypeStruct((1, ROWS, COLS), b...  72.2 us
    pallas_call x1, Pallas kernels, local(): pl.pallas_call(close, out_shape=(jax.ShapeDtypeStruct((1, ROWS, COLS), b1...  3.59 us

profile of v2, /device:TPU:1, one launch (start us, length us, event | category | flops | bytes accessed | tf_op | source)
XLA Modules:
  0.0 76.5 jit_solution(15018947245528892056)
XLA Ops:
  0.6 72.2 %shard_map.59 = (bf16[1,640,512]{2,1,0:T(8,128)(2,1)}, f32[5,8,128]{2,1,0:T(8,128)}) custom-call(bf16[1,144,5120]{2,1,0:T(8,128)(2,1)} %act.1, bf16[1,144,512]{2,1,0:T(8,128)(2,1)} %cot.1, f32[1,640,512]{2,1,0:T(8,128)} %mom.1, f32[128,128]{1,0:T(8,128)} %constant.2.clone.table), custom_call_target="tpu_custom_call" | custom-call | flops 2000000000 | bytes 6000000 | tf_op jit(solution)/shard_map/pallas_call | solution.py:453
  72.9 3.6 %shard_map.60 = (bf16[1,640,512]{2,1,0:T(8,128)(2,1)}, f32[640,512]{1,0:T(8,128)}) custom-call(f32[5,8,128]{2,1,0:T(8,128)} %get-tuple-element.4.bands, f32[128,128]{1,0:T(8,128)} %constant.2.clone.table, bf16[1,640,512]{2,1,0:T(8,128)(2,1)} %get-tuple-element.5.value), custom_call_target="tpu_custom_call" | custom-call | flops 500000000 | bytes 4000000 | tf_op jit(solution)/shard_map/pallas_call | solution.py:494

commit v3 on v2

--- a/solution.py
+++ b/solution.py
@@ -21,8 +21,8 @@
 N_REPLICA = NX * NYL * NZ
 CHUNK = 128
 NCHUNK = ROWS // CHUNK
-TILES = 5
-OWNER = NZ - TILES
+PIECES = 3
+PACKED = 16 * PIECES
 HIGH = lax.Precision.HIGHEST
 
 
@@ -56,9 +56,9 @@
     act, cot, mom, table,
     out_next, out_bands,
     act_v, buf_s, buf_g, cots, mom_v, tab, tab2, project, side_v, p_v, s_out, s_in, acc, next_v,
-    vec, xbuf, corebuf, zbuf, ybuf, fin,
-    go_sem, far_sem, load_sem, sem_s, sem_g, sem_c, send_sem, fwd_sem, s_send, s_recv, out_sem,
-    x_send, x_recv, core_sem, z_send, z_recv, y_send, y_recv, f_send, f_recv, g_send, g_recv,
+    vec, xbuf, mine, zbuf, ybuf, fin, fin_in,
+    go_sem, column_sem, load_sem, sem_s, sem_g, sem_c, send_sem, fwd_sem, s_send, s_recv, out_sem,
+    x_send, x_recv, z_send, z_recv, y_send, y_recv, f_send, f_recv,
 ):
     rep = lax.axis_index("replica")
     f = lax.axis_index("fsdp")
@@ -100,12 +100,30 @@
     for copy in loads:
         copy.start()
 
+    y = NYL * h + yl
+    ny = NYL * NH
+    place = lax.rem(y - NYL * x + ny, ny)
+
+    def lead_at(where):
+        where = lax.rem(where + 2 * ny, ny)
+        return jnp.where(jnp.logical_and(where >= 1, where <= 5), 1, 0)
+
+    lead_core = lead_at(place)
+    leads = c == lead_core
     barrier = pltpu.get_barrier_semaphore()
-    first_one = f == 0
-
-    @pl.when(jnp.logical_not(first_one))
+
+    def signal(sem, to):
+        pl.semaphore_signal(sem, inc=1, device_id=to, device_id_type=MESH)
+
+    @pl.when(jnp.logical_not(leads))
     def _():
-        pl.semaphore_signal(barrier, inc=1, device_id={"replica": rep, "fsdp": 0}, device_id_type=MESH)
+        signal(barrier, dev(h, lead_core))
+
+    for k in (-1, 1):
+        signal(barrier, dev(ring(h + k), lead_at(place + NYL * k)))
+    for k in range(1, NX):
+        xx = lax.rem(x + k, NX)
+        signal(barrier, dev(h, lead_at(y - NYL * xx), xx=xx))
 
     loads[0].wait()
     rows = tab[...]
@@ -115,13 +133,17 @@
     high, low = split(dot(rows, rows, 1, 1, HIGH))
     project[...] = jnp.concatenate([high, low], axis=1)
 
-    @pl.when(first_one)
+    tells = jnp.logical_and(place == 4, c == 0)
+    owns = jnp.logical_and(jnp.logical_not(leads), jnp.logical_or(place < 4, place > 5))
+    piece = jnp.where(c == 0, place - 1, lax.rem(ny - place, ny))
+
+    @pl.when(leads)
     def _():
-        pl.semaphore_wait(barrier, 2 * NH - 1)
-        for k in range(1, 2 * NH):
-            pl.semaphore_signal(go_sem, inc=1, device_id={"replica": rep, "fsdp": k}, device_id_type=MESH)
-
-    @pl.when(jnp.logical_not(first_one))
+        pl.semaphore_wait(barrier, 1 + 4 + 2 * (NX - 1))
+        signal(go_sem, dev(h, 1 - lead_core))
+        signal(barrier, dev(ring(x + 2), 0, yy=0))
+
+    @pl.when(jnp.logical_not(leads))
     def _():
         pl.semaphore_wait(go_sem, 1)
 
@@ -138,23 +160,13 @@
         remote(block(ring(h - 1), 0), buf_g.at[2 + c], send_sem.at[7], sem_g.at[2 + c], dev(ring(h - 1), 0)),
         remote(block(ring(h + 1), 1), buf_g.at[2 + c], send_sem.at[8], sem_g.at[2 + c], dev(ring(h + 1), 1)),
     ]
-    for copy in first:
+    for copy in first[:4] + second[:1]:
         copy.start()
 
-    far = [dev(h, c, xx=lax.rem(x + k, NX)) for k in range(1, NX)]
-
-    @pl.when(jnp.logical_not(first_one))
+    @pl.when(owns)
     def _():
-        for peer in far:
-            pl.semaphore_signal(barrier, inc=1, device_id=peer, device_id_type=MESH)
-        for k in range(NH):
-
-            @pl.when(k + c > 0)
-            def _():
-                pl.semaphore_signal(barrier, inc=1, device_id=dev(k, c, yy=1 - yl), device_id_type=MESH)
-
         def greet(k, carry):
-            pl.semaphore_signal(barrier, inc=1, device_id=dev(h, c, zz=lax.rem(z + k, NZ)), device_id_type=MESH)
+            signal(barrier, dev(h, c, zz=lax.rem(z + k, NZ)))
             return carry
 
         lax.fori_loop(1, NZ, greet, 0)
@@ -169,7 +181,7 @@
         return wide[:, :128] + wide[:, 128:] + dot(low, columns[:, :128], 1, 0)
 
     def pack(band):
-        return band[0:40] + pltpu.roll(band[40:80], 64, 1)
+        return jnp.concatenate([band[0:40] + pltpu.roll(band[40:80], 64, 1), jnp.zeros((8, 128), jnp.float32)], axis=0)
 
     q = dot(cots[2 + c], columns, 1, 0)
     q = q[:, :128] + q[:, 128:]
@@ -197,31 +209,25 @@
         remote(cots.at[c], cots.at[4 + c], fwd_sem.at[0], sem_c.at[4 + c], dev(h, oc)),
         remote(cots.at[4 + c], cots.at[c], fwd_sem.at[1], sem_c.at[c], dev(h, oc)),
     ]
-    first[0].wait_recv()
-    forwards[0].start()
-    first[1].wait_recv()
-    forwards[1].start()
-    first[0].wait_send()
-    first[1].wait_send()
-    for copy in second:
-        copy.start()
-
-    @pl.when(jnp.logical_not(first_one))
-    def _():
-        pl.semaphore_wait(barrier, len(far) + NZ - 1 + NH - 1 + c)
-
-    @pl.when(f == 1)
-    def _():
-        pl.semaphore_signal(far_sem, inc=1, device_id={"replica": rep, "fsdp": 0}, device_id_type=MESH)
-
-    @pl.when(first_one)
-    def _():
-        pl.semaphore_wait(far_sem, 1)
-
-    is_owner = z >= OWNER
-    tile = lax.rem(z + TILES, NZ)
-
-    mine = vec.at[2 * x + c]
+
+    def owner_y(xx, k):
+        return lax.rem(NYL * xx + jnp.where(c == 0, 1 + k, ny - k), ny)
+
+    def y_copy(k):
+        yy = owner_y(x, k)
+        return remote(mine.at[pl.ds(16 * k, 16)], ybuf.at[y], y_send.at[k], y_recv, dev(yy // NYL, c, yy=lax.rem(yy, NYL)))
+
+    def z_copy(k):
+        return remote(zbuf.at[z], zbuf.at[z], z_send.at[k], z_recv, dev(h, c, zz=lax.rem(z + k, NZ)))
+
+    f_targets = []
+    for xx in range(NX):
+        for yy in range(NYL):
+            here = jnp.logical_and(x == xx, jnp.logical_and(h == x, yl == yy))
+            f_targets.append((xx * NYL + yy, dev(x, c, xx=xx, yy=yy), here))
+
+    def f_copy(k, there):
+        return remote(fin.at[piece], fin_in.at[piece], f_send.at[k], f_recv.at[piece], there)
 
     def s_copy(k):
         at = pl.ds(pl.multiple_of(k * CHUNK, CHUNK), CHUNK)
@@ -237,36 +243,70 @@
         high, low = split(jnp.concatenate(rows, axis=0))
         return dot(jnp.concatenate([high, high], axis=1), columns, 1, 1) + dot(low, columns[:, :128], 1, 1)
 
-    def near_sums():
-        x_copies = []
+    def plane_sums():
+        copies = [remote(vec.at[2 * x + oc], xbuf.at[c], x_send.at[0], x_recv.at[c], dev(h, oc))]
         for k in range(1, NX):
-            to = lax.rem(x + k, NX)
-            x_copies.append(
-                remote(vec.at[pl.ds(2 * to, 2)], xbuf.at[k - 1], x_send.at[k - 1], x_recv.at[k - 1], dev(h, c, xx=to))
-            )
-        for copy in x_copies:
+            xx = lax.rem(x + k, NX)
+            for m in range(2):
+                copies.append(
+                    remote(vec.at[2 * xx + m], xbuf.at[2 * k + c], x_send.at[2 * k + m], x_recv.at[2 * k + c], dev(h, m, xx=xx))
+                )
+        for copy in copies:
             copy.start()
 
-        for copy in x_copies:
-            copy.wait()
-        vec[pl.ds(2 * x, 2)] = vec[pl.ds(2 * x, 2)] + (xbuf[0] + xbuf[1] + xbuf[2])
-
-        core_copy = remote(vec.at[2 * x + oc], corebuf, core_sem.at[0], core_sem.at[1], dev(h, oc))
-        core_copy.start()
-        core_copy.wait()
-        vec[2 * x + c] = vec[2 * x + c] + corebuf[...]
-
-        for t in range(TILES):
-            owner = OWNER + t
-            copy = remote(mine.at[pl.ds(8 * t, 8)], zbuf.at[z], z_send.at[t], z_recv, dev(h, c, zz=owner))
-
-            @pl.when(z == owner)
+        @pl.when(tells)
+        def _():
+            pl.semaphore_wait(barrier, ny)
+            for k in range(ny):
+                for m in range(2):
+                    if (k, m) != (0, 0):
+                        signal(column_sem, dev(ring(h + k // NYL), m, yy=k % NYL))
+
+        def arrived(slot):
+            pltpu.make_async_copy(xbuf.at[slot], xbuf.at[slot], x_recv.at[slot]).wait()
+
+        arrived(oc)
+        for slot in range(2, 2 * NX):
+            arrived(slot)
+        total = vec[2 * x + c] + xbuf[oc]
+        for slot in range(2, 2 * NX):
+            total = total + xbuf[slot]
+        mine[...] = total
+
+        @pl.when(jnp.logical_not(tells))
+        def _():
+            pl.semaphore_wait(column_sem, 1)
+
+        for k in range(PIECES):
+            copy = y_copy(k)
+            here = owner_y(x, k) == y
+
+            @pl.when(here)
             def _():
-                zbuf[owner] = mine[pl.ds(8 * t, 8)]
-
-            @pl.when(z != owner)
+                ybuf[y] = mine[pl.ds(16 * k, 16)]
+
+            @pl.when(jnp.logical_not(here))
             def _():
                 copy.start()
+
+        for copy in copies:
+            copy.wait_send()
+
+    def depth_sums():
+        @pl.when(owns)
+        def _():
+            pl.semaphore_wait(barrier, NZ - 1)
+            pltpu.make_async_copy(ybuf.at[pl.ds(0, ny - 1)], ybuf.at[pl.ds(0, ny - 1)], y_recv).wait()
+            total = ybuf[0]
+            for k in range(1, ny):
+                total = total + ybuf[k]
+            zbuf[z] = total
+
+            def go(k, carry):
+                z_copy(k).start()
+                return carry
+
+            lax.fori_loop(1, NZ, go, 0)
 
     def passed_on():
         loads[3].wait()
@@ -282,81 +322,38 @@
         for k in range(NCHUNK):
             s_copy(k).start()
 
-    def owner_sums():
-        for t in range(TILES):
-            owner = OWNER + t
-
-            @pl.when(z != owner)
+    def spread_sums():
+        for k in range(PIECES):
+
+            @pl.when(owner_y(x, k) != y)
             def _():
-                remote(mine.at[pl.ds(8 * t, 8)], zbuf.at[z], z_send.at[t], z_recv, dev(h, c, zz=owner)).wait_send()
-
-        def column_copy(yy):
-            return remote(zbuf.at[NZ], ybuf.at[h * NYL + yl], y_send.at[yy], y_recv, dev(x, c, yy=yy))
-
-        @pl.when(is_owner)
+                y_copy(k).wait_send()
+
+        @pl.when(owns)
         def _():
             pltpu.make_async_copy(zbuf.at[pl.ds(0, NZ - 1)], zbuf.at[pl.ds(0, NZ - 1)], z_recv).wait()
             total = zbuf[0]
             for k in range(1, NZ):
                 total = total + zbuf[k]
-            zbuf[NZ] = total
-            for yy in range(NYL):
-                here = jnp.logical_and(h == x, yl == yy)
-
-                @pl.when(here)
-                def _():
-                    ybuf[h * NYL + yl] = total
+            fin[piece] = total
+            for k, there, here in f_targets:
+                copy = f_copy(k, there)
 
                 @pl.when(jnp.logical_not(here))
                 def _():
-                    column_copy(yy).start()
-
-            for yy in range(NYL):
-                here = jnp.logical_and(h == x, yl == yy)
+                    copy.start()
+
+            def end(k, carry):
+                z_copy(k).wait_send()
+                return carry
+
+            lax.fori_loop(1, NZ, end, 0)
+            for k, there, here in f_targets:
+                copy = f_copy(k, there)
 
                 @pl.when(jnp.logical_not(here))
                 def _():
-                    column_copy(yy).wait_send()
-
-        def spread(k):
-            return remote(fin.at[tile], fin.at[tile], f_send.at[k], f_recv.at[tile], dev(h, c, zz=lax.rem(z + k, NZ)))
-
-        @pl.when(jnp.logical_and(is_owner, h == x))
-        def _():
-            pltpu.make_async_copy(ybuf.at[pl.ds(0, 7)], ybuf.at[pl.ds(0, 7)], y_recv).wait()
-            total = ybuf[0]
-            for k in range(1, NH * NYL):
-                total = total + ybuf[k]
-            fin[tile] = total
-
-            def go(k, carry):
-                spread(k).start()
-                return carry
-
-            lax.fori_loop(1, NZ, go, 0)
-
-            def end(k, carry):
-                spread(k).wait_send()
-                return carry
-
-            lax.fori_loop(1, NZ, end, 0)
-
-    def across_sums():
-        def across(k):
-            return remote(fin, fin, g_send.at[k - 1], g_recv, dev(h, c, xx=lax.rem(x + k, NX)))
-
-        @pl.when(h == x)
-        def _():
-            for t in range(TILES):
-
-                @pl.when(z != OWNER + t)
-                def _():
-                    pltpu.make_async_copy(fin.at[t], fin.at[t], f_recv.at[t]).wait()
-
-            for k in range(1, NX):
-                across(k).start()
-            for k in range(1, NX):
-                across(k).wait_send()
+                    copy.wait_send()
 
     def direct():
         loads[4].wait()
@@ -368,19 +365,32 @@
         acc[...] = DECAY * mom_v[...] + acc[...] - low_part(side_v[...] + sides(acc[...]))
 
     def bands_out():
-        @pl.when(h != x)
-        def _():
-            pltpu.make_async_copy(fin, fin, g_recv).wait()
-
-        bands_copy = pltpu.make_async_copy(fin, out_bands, out_sem.at[NCHUNK])
+        for k in range(PIECES):
+            here = jnp.logical_and(h == x, owner_y(h, k) == y)
+
+            @pl.when(jnp.logical_not(here))
+            def _():
+                pltpu.make_async_copy(fin_in.at[k], fin_in.at[k], f_recv.at[k]).wait()
+
+            @pl.when(here)
+            def _():
+                fin_in[k] = fin[k]
+
+        bands_copy = pltpu.make_async_copy(fin_in, out_bands, out_sem.at[NCHUNK])
         bands_copy.start()
         bands_copy.wait()
 
-    near_sums()
+    plane_sums()
+    for copy in first[4:] + second[1:]:
+        copy.start()
+    first[0].wait_recv()
+    forwards[0].start()
+    first[1].wait_recv()
+    forwards[1].start()
+    depth_sums()
     passed_on()
-    owner_sums()
+    spread_sums()
     direct()
-    across_sums()
 
     def out_copy(k):
         at = pl.ds(pl.multiple_of(k * CHUNK, CHUNK), CHUNK)
@@ -402,15 +412,15 @@
         return carry
 
     lax.fori_loop(0, NCHUNK, drain, 0)
-    for copy in first[2:] + second + forwards:
+    for copy in first + second + forwards:
         copy.wait_send()
 
 
 def close(bands, table, value, out_next, out_update, update_v, value_v, sem):
     held = pltpu.make_async_copy(value, value_v, sem.at[NCHUNK])
     held.start()
-    total = bands[...].reshape(8 * TILES, 128) * (1.0 / N_REPLICA)
-    left = lax.broadcasted_iota(jnp.int32, (8 * TILES, 128), 1) < 64
+    total = bands[...].reshape(PACKED, 128)[0:40] * (1.0 / N_REPLICA)
+    left = lax.broadcasted_iota(jnp.int32, (40, 128), 1) < 64
     upper = jnp.where(left, total, 0.0)
     lower = jnp.where(left, pltpu.roll(total, 64, 1), 0.0)
     shared = jnp.concatenate([upper, lower, jnp.zeros((48, 128), jnp.float32)], axis=0)
@@ -454,7 +464,7 @@
             kernel,
             out_shape=(
                 jax.ShapeDtypeStruct((1, ROWS, COLS), b16),
-                jax.ShapeDtypeStruct((TILES, 8, 128), f32),
+                jax.ShapeDtypeStruct((PIECES, 16, 128), f32),
             ),
             in_specs=[pl.BlockSpec(memory_space=pl.ANY)] * 4,
             out_specs=(pl.BlockSpec(memory_space=pl.ANY),) * 2,
@@ -473,18 +483,18 @@
                 pltpu.VMEM((ROWS, COLS), b16),
                 pltpu.VMEM((ROWS, COLS), f32),
                 pltpu.VMEM((ROWS, COLS), b16),
-                pltpu.VMEM((2 * NH, 8 * TILES, 128), f32),
-                pltpu.VMEM((NX - 1, 2, 8 * TILES, 128), f32),
-                pltpu.VMEM((8 * TILES, 128), f32),
-                pltpu.VMEM((NZ + 1, 8, 128), f32),
-                pltpu.VMEM((NH * NYL, 8, 128), f32),
-                pltpu.VMEM((TILES, 8, 128), f32),
+                pltpu.VMEM((2 * NH, PACKED, 128), f32),
+                pltpu.VMEM((2 * NX, PACKED, 128), f32),
+                pltpu.VMEM((PACKED, 128), f32),
+                pltpu.VMEM((NZ, 16, 128), f32),
+                pltpu.VMEM((NH * NYL, 16, 128), f32),
+                pltpu.VMEM((PIECES, 16, 128), f32),
+                pltpu.VMEM((PIECES, 16, 128), f32),
                 pltpu.SemaphoreType.REGULAR, pltpu.SemaphoreType.REGULAR,
                 dma((5 + 2 * NH,)), dma((4,)), dma((4,)), dma((6,)), dma((9,)), dma((2,)),
                 dma((NCHUNK,)), dma((NCHUNK,)), dma((NCHUNK + 1,)),
-                dma((NX - 1,)), dma((NX - 1,)), dma((2,)),
-                dma((TILES,)), dma, dma((NYL,)), dma,
-                dma((NZ,)), dma((TILES,)), dma((NX - 1,)), dma,
+                dma((2 * NX,)), dma((2 * NX,)),
+                dma((NZ,)), dma, dma((PIECES,)), dma, dma((NX * NYL,)), dma((PIECES,)),
             ],
             compiler_params=pltpu.CompilerParams(
                 collective_id=0, has_side_effects=True, vmem_limit_bytes=60 * 1024 * 1024

time: 77.4 us -> 60.7 us (0.78)
  Pallas kernels: 75.8 us -> 59.8 us
    pallas_call x1, Pallas kernels: 72.2 us -> 56.2 us  [local(): pl.pallas_call(kernel, out_shape=(jax.ShapeDtypeStruct((1, ROWS, COLS), b...]
where the time goes in v3:
time: 60.7 us; the launch traced here: 60.4 us
  Pallas kernels  59.8 us (99%)
  between operations  0.64 us (1%)
    pallas_call x1, Pallas kernels, local(): pl.pallas_call(kernel, out_shape=(jax.ShapeDtypeStruct((1, ROWS, COLS), b...  56.2 us
    pallas_call x1, Pallas kernels, local(): pl.pallas_call(close, out_shape=(jax.ShapeDtypeStruct((1, ROWS, COLS), b1...  3.59 us

profile of v3, /device:TPU:1, one launch (start us, length us, event | category | flops | bytes accessed | tf_op | source)
XLA Modules:
  0.0 60.4 jit_solution(10793009099818652058)
XLA Ops:
  0.6 56.2 %shard_map.59 = (bf16[1,640,512]{2,1,0:T(8,128)(2,1)}, f32[3,16,128]{2,1,0:T(8,128)}) custom-call(bf16[1,144,5120]{2,1,0:T(8,128)(2,1)} %act.1, bf16[1,144,512]{2,1,0:T(8,128)(2,1)} %cot.1, f32[1,640,512]{2,1,0:T(8,128)} %mom.1, f32[128,128]{1,0:T(8,128)} %constant.2.clone.table), custom_call_target="tpu_custom_call" | custom-call | flops 2000000000 | bytes 6000000 | tf_op jit(solution)/shard_map/pallas_call | solution.py:463
  56.9 3.6 %shard_map.60 = (bf16[1,640,512]{2,1,0:T(8,128)(2,1)}, f32[640,512]{1,0:T(8,128)}) custom-call(f32[3,16,128]{2,1,0:T(8,128)} %get-tuple-element.4.bands, f32[128,128]{1,0:T(8,128)} %constant.2.clone.table, bf16[1,640,512]{2,1,0:T(8,128)(2,1)} %get-tuple-element.5.value), custom_call_target="tpu_custom_call" | custom-call | flops 500000000 | bytes 4000000 | tf_op jit(solution)/shard_map/pallas_call | solution.py:504

commit v4 on v3

--- a/solution.py
+++ b/solution.py
@@ -20,6 +20,8 @@
 NX, NYL, NZ, NH = 4, 2, 16, 4
 N_REPLICA = NX * NYL * NZ
 CHUNK = 128
+CUT = 16
+EARLY = 4
 NCHUNK = ROWS // CHUNK
 PIECES = 3
 PACKED = 16 * PIECES
@@ -147,20 +149,28 @@
     def _():
         pl.semaphore_wait(go_sem, 1)
 
+    def via(core, low, high, sem):
+        start = pl.multiple_of((ring(h + 2) * 2 + core) * ROWS, ROWS)
+        part = act.at[0, pl.ds(low, high - low), pl.ds(start, ROWS)]
+        to = dev(ring(h + 1 - 2 * core), core)
+        return remote(part, buf_s.at[c, pl.ds(low, high - low)], send_sem.at[sem], sem_s.at[c], to)
+
     first = [
         remote(cot.at[0], cots.at[c], send_sem.at[0], sem_c.at[c], dev(ring(h + s), c)),
         remote(cot.at[0], cots.at[4 + c], send_sem.at[1], sem_c.at[4 + c], dev(ring(h - s), c)),
         remote(cot.at[0], cots.at[2 + c], send_sem.at[2], sem_c.at[2 + c], dev(h, oc)),
         remote(block(ring(h + s * -1), oc), buf_s.at[2 + c], send_sem.at[3], sem_s.at[2 + c], dev(h, oc)),
-        remote(block(ring(h + 2), 0), buf_s.at[c], send_sem.at[4], sem_s.at[c], dev(ring(h + 1), 0)),
-        remote(block(ring(h + 2), 1), buf_s.at[c], send_sem.at[5], sem_s.at[c], dev(ring(h - 1), 1)),
+        via(0, 0, CUT, 4),
+        via(1, 0, CUT, 5),
     ]
     second = [
+        via(0, CUT, T, 9),
+        via(1, CUT, T, 10),
         remote(block(h, oc), buf_g.at[c], send_sem.at[6], sem_g.at[c], dev(h, oc)),
         remote(block(ring(h - 1), 0), buf_g.at[2 + c], send_sem.at[7], sem_g.at[2 + c], dev(ring(h - 1), 0)),
         remote(block(ring(h + 1), 1), buf_g.at[2 + c], send_sem.at[8], sem_g.at[2 + c], dev(ring(h + 1), 1)),
     ]
-    for copy in first[:4] + second[:1]:
+    for copy in first + second[2:3]:
         copy.start()
 
     @pl.when(owns)
@@ -243,7 +253,7 @@
         high, low = split(jnp.concatenate(rows, axis=0))
         return dot(jnp.concatenate([high, high], axis=1), columns, 1, 1) + dot(low, columns[:, :128], 1, 1)
 
-    def plane_sums():
+    def plane_copies():
         copies = [remote(vec.at[2 * x + oc], xbuf.at[c], x_send.at[0], x_recv.at[c], dev(h, oc))]
         for k in range(1, NX):
             xx = lax.rem(x + k, NX)
@@ -251,8 +261,10 @@
                 copies.append(
                     remote(vec.at[2 * xx + m], xbuf.at[2 * k + c], x_send.at[2 * k + m], x_recv.at[2 * k + c], dev(h, m, xx=xx))
                 )
-        for copy in copies:
-            copy.start()
+        return copies
+
+    def plane_sums():
+        copies = plane_copies()
 
         @pl.when(tells)
         def _():
@@ -302,11 +314,8 @@
                 total = total + ybuf[k]
             zbuf[z] = total
 
-            def go(k, carry):
+            for k in sorted(range(1, NZ), key=lambda k: abs(k - NZ // 2)):
                 z_copy(k).start()
-                return carry
-
-            lax.fori_loop(1, NZ, go, 0)
 
     def passed_on():
         loads[3].wait()
@@ -380,15 +389,36 @@
         bands_copy.start()
         bands_copy.wait()
 
-    plane_sums()
-    for copy in first[4:] + second[1:]:
+    def bulk():
+        for copy in second[:2] + second[3:]:
+            copy.start()
+
+    def hand_on():
+        first[0].wait_recv()
+        forwards[0].start()
+        first[1].wait_recv()
+        forwards[1].start()
+
+    for copy in plane_copies():
         copy.start()
-    first[0].wait_recv()
-    forwards[0].start()
-    first[1].wait_recv()
-    forwards[1].start()
-    depth_sums()
-    passed_on()
+    early = z < EARLY
+
+    @pl.when(early)
+    def _():
+        bulk()
+        hand_on()
+        plane_sums()
+        passed_on()
+        depth_sums()
+
+    @pl.when(jnp.logical_not(early))
+    def _():
+        plane_sums()
+        bulk()
+        hand_on()
+        depth_sums()
+        passed_on()
+
     spread_sums()
     direct()
 
@@ -416,10 +446,16 @@
         copy.wait_send()
 
 
-def close(bands, table, value, out_next, out_update, update_v, value_v, sem):
-    held = pltpu.make_async_copy(value, value_v, sem.at[NCHUNK])
-    held.start()
-    total = bands[...].reshape(PACKED, 128)[0:40] * (1.0 / N_REPLICA)
+def close(bands, table, value, out_next, out_update, bands_v, table_v, update_v, value_v, sem):
+    given = [
+        pltpu.make_async_copy(bands, bands_v, sem.at[NCHUNK + 1]),
+        pltpu.make_async_copy(table, table_v, sem.at[NCHUNK + 2]),
+        pltpu.make_async_copy(value, value_v, sem.at[NCHUNK]),
+    ]
+    for each in given:
+        each.start()
+    given[0].wait()
+    total = bands_v[...].reshape(PACKED, 128)[0:40] * (1.0 / N_REPLICA)
     left = lax.broadcasted_iota(jnp.int32, (40, 128), 1) < 64
     upper = jnp.where(left, total, 0.0)
     lower = jnp.where(left, pltpu.roll(total, 64, 1), 0.0)
@@ -427,12 +463,19 @@
     row = lax.broadcasted_iota(jnp.int32, (128, 128), 0) // BAND
     col = lax.broadcasted_iota(jnp.int32, (128, 128), 1) // BAND
     same = (row == col).astype(jnp.float32)
-    power = dot(dot(same, shared * shared, 1, 0, HIGH), same, 1, 0, HIGH) * (1.0 / (SPAN * SPAN))
-    shared = shared / jnp.sqrt(power + EPS)
-    held.wait()
+    same = same.astype(jnp.bfloat16)
+
+    def both(value):
+        return jnp.concatenate(split(value), axis=1)
+
+    power = dot(same, both(shared * shared), 1, 0)
+    power = dot(both(power[:, :128] + power[:, 128:]), jnp.concatenate([same, same], axis=0), 1, 0)
+    shared = shared / jnp.sqrt(power * (1.0 / (SPAN * SPAN)) + EPS)
+    given[2].wait()
     copy = pltpu.make_async_copy(value_v, out_next, sem.at[NCHUNK])
     copy.start()
-    rows = table[...]
+    given[1].wait()
+    rows = table_v[...]
     columns = [split(turn(rows, 2 * BAND * k)) for k in range(COLS // CHUNK)]
     high, low = split(shared)
     left, right = jnp.concatenate([high, high], axis=1), low
@@ -491,7 +534,7 @@
                 pltpu.VMEM((PIECES, 16, 128), f32),
                 pltpu.VMEM((PIECES, 16, 128), f32),
                 pltpu.SemaphoreType.REGULAR, pltpu.SemaphoreType.REGULAR,
-                dma((5 + 2 * NH,)), dma((4,)), dma((4,)), dma((6,)), dma((9,)), dma((2,)),
+                dma((5 + 2 * NH,)), dma((4,)), dma((4,)), dma((6,)), dma((11,)), dma((2,)),
                 dma((NCHUNK,)), dma((NCHUNK,)), dma((NCHUNK + 1,)),
                 dma((2 * NX,)), dma((2 * NX,)),
                 dma((NZ,)), dma, dma((PIECES,)), dma, dma((NX * NYL,)), dma((PIECES,)),
@@ -507,9 +550,15 @@
                 jax.ShapeDtypeStruct((1, ROWS, COLS), b16),
                 jax.ShapeDtypeStruct((ROWS, COLS), f32),
             ),
-            in_specs=[pl.BlockSpec(memory_space=pltpu.VMEM)] * 2 + [pl.BlockSpec(memory_space=pl.ANY)],
+            in_specs=[pl.BlockSpec(memory_space=pl.ANY)] * 3,
             out_specs=(pl.BlockSpec(memory_space=pl.ANY),) * 2,
-            scratch_shapes=[pltpu.VMEM((ROWS, COLS), f32), pltpu.VMEM((1, ROWS, COLS), b16), dma((NCHUNK + 1,))],
+            scratch_shapes=[
+                pltpu.VMEM((PIECES, 16, 128), f32),
+                pltpu.VMEM((CHUNK, 128), f32),
+                pltpu.VMEM((ROWS, COLS), f32),
+                pltpu.VMEM((1, ROWS, COLS), b16),
+                dma((NCHUNK + 3,)),
+            ],
             compiler_params=pltpu.CompilerParams(vmem_limit_bytes=60 * 1024 * 1024),
             cost_estimate=pl.CostEstimate(flops=500_000_000, bytes_accessed=4_000_000, transcendentals=0),
         )(bands, rows, value)

time: 60.7 us -> 55 us (0.906); the launches traced: 60.4 us -> 54 us
  Pallas kernels: 59.8 us -> 53.3 us
    pallas_call x1, Pallas kernels: 56.2 us -> 50.5 us  [local(): pl.pallas_call(kernel, out_shape=(jax.ShapeDtypeStruct((1, ROWS, COLS), b...]
    pallas_call x1, Pallas kernels: 3.59 us -> 2.81 us  [local(): pl.pallas_call(close, out_shape=(jax.ShapeDtypeStruct((1, ROWS, COLS), b1...]
where the time goes in v4:
time: 55 us; the launch traced here: 54 us
  Pallas kernels  53.3 us (97%)
  between operations  0.64 us (1%)
    pallas_call x1, Pallas kernels, local(): pl.pallas_call(kernel, out_shape=(jax.ShapeDtypeStruct((1, ROWS, COLS), b...  50.5 us
    pallas_call x1, Pallas kernels, local(): pl.pallas_call(close, out_shape=(jax.ShapeDtypeStruct((1, ROWS, COLS), b1...  2.81 us

profile of v4, /device:TPU:1, one launch (start us, length us, event | category | flops | bytes accessed | tf_op | source)
XLA Modules:
  0.0 54.0 jit_solution(3825594063200031412)
XLA Ops:
  0.6 50.5 %shard_map.59 = (bf16[1,640,512]{2,1,0:T(8,128)(2,1)}, f32[3,16,128]{2,1,0:T(8,128)}) custom-call(bf16[1,144,5120]{2,1,0:T(8,128)(2,1)} %act.1, bf16[1,144,512]{2,1,0:T(8,128)(2,1)} %cot.1, f32[1,640,512]{2,1,0:T(8,128)} %mom.1, f32[128,128]{1,0:T(8,128)} %constant.2.clone.table), custom_call_target="tpu_custom_call" | custom-call | flops 2000000000 | bytes 6000000 | tf_op jit(solution)/shard_map/pallas_call | solution.py:506
  51.2 2.8 %shard_map.60 = (bf16[1,640,512]{2,1,0:T(8,128)(2,1)}, f32[640,512]{1,0:T(8,128)}) custom-call(f32[3,16,128]{2,1,0:T(8,128)} %get-tuple-element.4.bands, f32[128,128]{1,0:T(8,128)} %constant.2.clone.table, bf16[1,640,512]{2,1,0:T(8,128)(2,1)} %get-tuple-element.5.value), custom_call_target="tpu_custom_call" | custom-call | flops 500000000 | bytes 4000000 | tf_op jit(solution)/shard_map/pallas_call | solution.py:547

commit v5 on v4

--- a/solution.py
+++ b/solution.py
@@ -88,6 +88,31 @@
         start = pl.multiple_of((hh * 2 + cc) * ROWS, ROWS)
         return act.at[0, :, pl.ds(start, ROWS)]
 
+    y = NYL * h + yl
+    ny = NYL * NH
+    place = lax.rem(y - NYL * x + ny, ny)
+
+    def lead_at(where):
+        where = lax.rem(where + 2 * ny, ny)
+        return jnp.where(jnp.logical_and(where >= 1, where <= 5), 1, 0)
+
+    lead_core = lead_at(place)
+    leads = c == lead_core
+    barrier = pltpu.get_barrier_semaphore()
+
+    def signal(sem, to):
+        pl.semaphore_signal(sem, inc=1, device_id=to, device_id_type=MESH)
+
+    @pl.when(jnp.logical_not(leads))
+    def _():
+        signal(barrier, dev(h, lead_core))
+
+    for k in (-1, 1):
+        signal(barrier, dev(ring(h + k), lead_at(place + NYL * k)))
+    for k in range(1, NX):
+        xx = lax.rem(x + k, NX)
+        signal(barrier, dev(h, lead_at(y - NYL * xx), xx=xx))
+
     loads = [
         pltpu.make_async_copy(table, tab, load_sem.at[0]),
         pltpu.make_async_copy(cot.at[0], cots.at[2 + c], load_sem.at[1]),
@@ -102,30 +127,51 @@
     for copy in loads:
         copy.start()
 
-    y = NYL * h + yl
-    ny = NYL * NH
-    place = lax.rem(y - NYL * x + ny, ny)
-
-    def lead_at(where):
-        where = lax.rem(where + 2 * ny, ny)
-        return jnp.where(jnp.logical_and(where >= 1, where <= 5), 1, 0)
-
-    lead_core = lead_at(place)
-    leads = c == lead_core
-    barrier = pltpu.get_barrier_semaphore()
-
-    def signal(sem, to):
-        pl.semaphore_signal(sem, inc=1, device_id=to, device_id_type=MESH)
+    tells = jnp.logical_and(place == 4, c == 0)
+    owns = jnp.logical_and(jnp.logical_not(leads), jnp.logical_or(place < 4, place > 5))
+    piece = jnp.where(c == 0, place - 1, lax.rem(ny - place, ny))
+
+    @pl.when(leads)
+    def _():
+        pl.semaphore_wait(barrier, 1 + 4 + 2 * (NX - 1))
+        signal(go_sem, dev(h, 1 - lead_core))
+        signal(barrier, dev(ring(x + 2), 0, yy=0))
 
     @pl.when(jnp.logical_not(leads))
     def _():
-        signal(barrier, dev(h, lead_core))
-
-    for k in (-1, 1):
-        signal(barrier, dev(ring(h + k), lead_at(place + NYL * k)))
-    for k in range(1, NX):
-        xx = lax.rem(x + k, NX)
-        signal(barrier, dev(h, lead_at(y - NYL * xx), xx=xx))
+        pl.semaphore_wait(go_sem, 1)
+
+    def via(core, low, high, sem):
+        start = pl.multiple_of((ring(h + 2) * 2 + core) * ROWS, ROWS)
+        part = act.at[0, pl.ds(low, high - low), pl.ds(start, ROWS)]
+        to = dev(ring(h + 1 - 2 * core), core)
+        return remote(part, buf_s.at[c, pl.ds(low, high - low)], send_sem.at[sem], sem_s.at[c], to)
+
+    first = [
+        remote(cot.at[0], cots.at[c], send_sem.at[0], sem_c.at[c], dev(ring(h + s), c)),
+        remote(cot.at[0], cots.at[4 + c], send_sem.at[1], sem_c.at[4 + c], dev(ring(h - s), c)),
+        remote(cot.at[0], cots.at[2 + c], send_sem.at[2], sem_c.at[2 + c], dev(h, oc)),
+        remote(block(ring(h + s * -1), oc), buf_s.at[2 + c], send_sem.at[3], sem_s.at[2 + c], dev(h, oc)),
+        via(0, 0, CUT, 4),
+        via(1, 0, CUT, 5),
+    ]
+    second = [
+        via(0, CUT, T, 9),
+        via(1, CUT, T, 10),
+        remote(block(h, oc), buf_g.at[c], send_sem.at[6], sem_g.at[c], dev(h, oc)),
+        remote(block(ring(h - 1), 0), buf_g.at[2 + c], send_sem.at[7], sem_g.at[2 + c], dev(ring(h - 1), 0)),
+        remote(block(ring(h + 1), 1), buf_g.at[2 + c], send_sem.at[8], sem_g.at[2 + c], dev(ring(h + 1), 1)),
+    ]
+    for copy in first + second[2:3]:
+        copy.start()
+
+    @pl.when(owns)
+    def _():
+        def greet(k, carry):
+            signal(barrier, dev(h, c, zz=lax.rem(z + k, NZ)))
+            return carry
+
+        lax.fori_loop(1, NZ, greet, 0)
 
     loads[0].wait()
     rows = tab[...]
@@ -134,52 +180,6 @@
         tab2[k * CHUNK : (k + 1) * CHUNK] = jnp.concatenate([high, low], axis=1)
     high, low = split(dot(rows, rows, 1, 1, HIGH))
     project[...] = jnp.concatenate([high, low], axis=1)
-
-    tells = jnp.logical_and(place == 4, c == 0)
-    owns = jnp.logical_and(jnp.logical_not(leads), jnp.logical_or(place < 4, place > 5))
-    piece = jnp.where(c == 0, place - 1, lax.rem(ny - place, ny))
-
-    @pl.when(leads)
-    def _():
-        pl.semaphore_wait(barrier, 1 + 4 + 2 * (NX - 1))
-        signal(go_sem, dev(h, 1 - lead_core))
-        signal(barrier, dev(ring(x + 2), 0, yy=0))
-
-    @pl.when(jnp.logical_not(leads))
-    def _():
-        pl.semaphore_wait(go_sem, 1)
-
-    def via(core, low, high, sem):
-        start = pl.multiple_of((ring(h + 2) * 2 + core) * ROWS, ROWS)
-        part = act.at[0, pl.ds(low, high - low), pl.ds(start, ROWS)]
-        to = dev(ring(h + 1 - 2 * core), core)
-        return remote(part, buf_s.at[c, pl.ds(low, high - low)], send_sem.at[sem], sem_s.at[c], to)
-
-    first = [
-        remote(cot.at[0], cots.at[c], send_sem.at[0], sem_c.at[c], dev(ring(h + s), c)),
-        remote(cot.at[0], cots.at[4 + c], send_sem.at[1], sem_c.at[4 + c], dev(ring(h - s), c)),
-        remote(cot.at[0], cots.at[2 + c], send_sem.at[2], sem_c.at[2 + c], dev(h, oc)),
-        remote(block(ring(h + s * -1), oc), buf_s.at[2 + c], send_sem.at[3], sem_s.at[2 + c], dev(h, oc)),
-        via(0, 0, CUT, 4),
-        via(1, 0, CUT, 5),
-    ]
-    second = [
-        via(0, CUT, T, 9),
-        via(1, CUT, T, 10),
-        remote(block(h, oc), buf_g.at[c], send_sem.at[6], sem_g.at[c], dev(h, oc)),
-        remote(block(ring(h - 1), 0), buf_g.at[2 + c], send_sem.at[7], sem_g.at[2 + c], dev(ring(h - 1), 0)),
-        remote(block(ring(h + 1), 1), buf_g.at[2 + c], send_sem.at[8], sem_g.at[2 + c], dev(ring(h + 1), 1)),
-    ]
-    for copy in first + second[2:3]:
-        copy.start()
-
-    @pl.when(owns)
-    def _():
-        def greet(k, carry):
-            signal(barrier, dev(h, c, zz=lax.rem(z + k, NZ)))
-            return carry
-
-        lax.fori_loop(1, NZ, greet, 0)
 
     for copy in loads[1:3] + loads[5:]:
         copy.wait()

time: 55 us -> 54.1 us (0.984); the launches traced: 54 us -> 53.9 us
  no operation moved by 1% of the time
where the time goes in v5:
time: 54.1 us; the launch traced here: 53.9 us
  Pallas kernels  53.3 us (99%)
  between operations  0.64 us (1%)
    pallas_call x1, Pallas kernels, local(): pl.pallas_call(kernel, out_shape=(jax.ShapeDtypeStruct((1, ROWS, COLS), b...  50.5 us
    pallas_call x1, Pallas kernels, local(): pl.pallas_call(close, out_shape=(jax.ShapeDtypeStruct((1, ROWS, COLS), b1...  2.81 us

profile of v5, /device:TPU:1, one launch (start us, length us, event | category | flops | bytes accessed | tf_op | source)
XLA Modules:
  0.0 53.9 jit_solution(2134900154339659176)
XLA Ops:
  0.6 50.5 %shard_map.59 = (bf16[1,640,512]{2,1,0:T(8,128)(2,1)}, f32[3,16,128]{2,1,0:T(8,128)}) custom-call(bf16[1,144,5120]{2,1,0:T(8,128)(2,1)} %act.1, bf16[1,144,512]{2,1,0:T(8,128)(2,1)} %cot.1, f32[1,640,512]{2,1,0:T(8,128)} %mom.1, f32[128,128]{1,0:T(8,128)} %constant.2.clone.table), custom_call_target="tpu_custom_call" | custom-call | flops 2000000000 | bytes 6000000 | tf_op jit(solution)/shard_map/pallas_call | solution.py:506
  51.1 2.8 %shard_map.60 = (bf16[1,640,512]{2,1,0:T(8,128)(2,1)}, f32[640,512]{1,0:T(8,128)}) custom-call(f32[3,16,128]{2,1,0:T(8,128)} %get-tuple-element.4.bands, f32[128,128]{1,0:T(8,128)} %constant.2.clone.table, bf16[1,640,512]{2,1,0:T(8,128)(2,1)} %get-tuple-element.5.value), custom_call_target="tpu_custom_call" | custom-call | flops 500000000 | bytes 4000000 | tf_op jit(solution)/shard_map/pallas_call | solution.py:547

commit v6 on v5

--- a/solution.py
+++ b/solution.py
@@ -58,7 +58,7 @@
     act, cot, mom, table,
     out_next, out_bands,
     act_v, buf_s, buf_g, cots, mom_v, tab, tab2, project, side_v, p_v, s_out, s_in, acc, next_v,
-    vec, xbuf, mine, zbuf, ybuf, fin, fin_in,
+    vec, xbuf, mine, zbuf, ybuf, fin, fin_in, shared_v,
     go_sem, column_sem, load_sem, sem_s, sem_g, sem_c, send_sem, fwd_sem, s_send, s_recv, out_sem,
     x_send, x_recv, z_send, z_recv, y_send, y_recv, f_send, f_recv,
 ):
@@ -373,6 +373,8 @@
         acc[...] = dot(buf_g[...].reshape(4 * T, ROWS), cots[2:6].reshape(4 * T, COLS), 0, 0)
         acc[...] = DECAY * mom_v[...] + acc[...] - low_part(side_v[...] + sides(acc[...]))
 
+    bands_copy = pltpu.make_async_copy(shared_v, out_bands, out_sem.at[NCHUNK])
+
     def bands_out():
         for k in range(PIECES):
             here = jnp.logical_and(h == x, owner_y(h, k) == y)
@@ -385,9 +387,23 @@
             def _():
                 fin_in[k] = fin[k]
 
-        bands_copy = pltpu.make_async_copy(fin_in, out_bands, out_sem.at[NCHUNK])
+        total = fin_in[...].reshape(PACKED, 128)[0:40] * (1.0 / N_REPLICA)
+        left = lax.broadcasted_iota(jnp.int32, (40, 128), 1) < 64
+        upper = jnp.where(left, total, 0.0)
+        lower = jnp.where(left, pltpu.roll(total, 64, 1), 0.0)
+        shared = jnp.concatenate([upper, lower, jnp.zeros((48, 128), jnp.float32)], axis=0)
+        row = lax.broadcasted_iota(jnp.int32, (128, 128), 0) // BAND
+        col = lax.broadcasted_iota(jnp.int32, (128, 128), 1) // BAND
+        same = (row == col).astype(jnp.float32)
+        same = same.astype(jnp.bfloat16)
+
+        def both(value):
+            return jnp.concatenate(split(value), axis=1)
+
+        power = dot(same, both(shared * shared), 1, 0)
+        power = dot(both(power[:, :128] + power[:, 128:]), jnp.concatenate([same, same], axis=0), 1, 0)
+        shared_v[...] = shared / jnp.sqrt(power * (1.0 / (SPAN * SPAN)) + EPS)
         bands_copy.start()
-        bands_copy.wait()
 
     def bulk():
         for copy in second[:2] + second[3:]:
@@ -433,8 +449,9 @@
         out_copy(k).start()
         return carry
 
+    pl.when(jnp.logical_not(early))(bands_out)
     lax.fori_loop(0, NCHUNK, finish, 0)
-    bands_out()
+    pl.when(early)(bands_out)
 
     def drain(k, carry):
         s_copy(k).wait_send()
@@ -442,6 +459,7 @@
         return carry
 
     lax.fori_loop(0, NCHUNK, drain, 0)
+    bands_copy.wait()
     for copy in first + second + forwards:
         copy.wait_send()
 
@@ -455,22 +473,7 @@
     for each in given:
         each.start()
     given[0].wait()
-    total = bands_v[...].reshape(PACKED, 128)[0:40] * (1.0 / N_REPLICA)
-    left = lax.broadcasted_iota(jnp.int32, (40, 128), 1) < 64
-    upper = jnp.where(left, total, 0.0)
-    lower = jnp.where(left, pltpu.roll(total, 64, 1), 0.0)
-    shared = jnp.concatenate([upper, lower, jnp.zeros((48, 128), jnp.float32)], axis=0)
-    row = lax.broadcasted_iota(jnp.int32, (128, 128), 0) // BAND
-    col = lax.broadcasted_iota(jnp.int32, (128, 128), 1) // BAND
-    same = (row == col).astype(jnp.float32)
-    same = same.astype(jnp.bfloat16)
-
-    def both(value):
-        return jnp.concatenate(split(value), axis=1)
-
-    power = dot(same, both(shared * shared), 1, 0)
-    power = dot(both(power[:, :128] + power[:, 128:]), jnp.concatenate([same, same], axis=0), 1, 0)
-    shared = shared / jnp.sqrt(power * (1.0 / (SPAN * SPAN)) + EPS)
+    shared = bands_v[...]
     given[2].wait()
     copy = pltpu.make_async_copy(value_v, out_next, sem.at[NCHUNK])
     copy.start()
@@ -507,7 +510,7 @@
             kernel,
             out_shape=(
                 jax.ShapeDtypeStruct((1, ROWS, COLS), b16),
-                jax.ShapeDtypeStruct((PIECES, 16, 128), f32),
+                jax.ShapeDtypeStruct((128, 128), f32),
             ),
             in_specs=[pl.BlockSpec(memory_space=pl.ANY)] * 4,
             out_specs=(pl.BlockSpec(memory_space=pl.ANY),) * 2,
@@ -533,6 +536,7 @@
                 pltpu.VMEM((NH * NYL, 16, 128), f32),
                 pltpu.VMEM((PIECES, 16, 128), f32),
                 pltpu.VMEM((PIECES, 16, 128), f32),
+                pltpu.VMEM((128, 128), f32),
                 pltpu.SemaphoreType.REGULAR, pltpu.SemaphoreType.REGULAR,
                 dma((5 + 2 * NH,)), dma((4,)), dma((4,)), dma((6,)), dma((11,)), dma((2,)),
                 dma((NCHUNK,)), dma((NCHUNK,)), dma((NCHUNK + 1,)),
@@ -553,7 +557,7 @@
             in_specs=[pl.BlockSpec(memory_space=pl.ANY)] * 3,
             out_specs=(pl.BlockSpec(memory_space=pl.ANY),) * 2,
             scratch_shapes=[
-                pltpu.VMEM((PIECES, 16, 128), f32),
+                pltpu.VMEM((128, 128), f32),
                 pltpu.VMEM((CHUNK, 128), f32),
                 pltpu.VMEM((ROWS, COLS), f32),
                 pltpu.VMEM((1, ROWS, COLS), b16),

time: 54.1 us -> 54.5 us (level)
  no operation moved by 1% of the time
where the time goes in v6:
time: 54.5 us; the launch traced here: 54.3 us
  Pallas kernels  53.7 us (99%)
  between operations  0.64 us (1%)
    pallas_call x1, Pallas kernels, local(): pl.pallas_call(kernel, out_shape=(jax.ShapeDtypeStruct((1, ROWS, COLS), b...  50.9 us
    pallas_call x1, Pallas kernels, local(): pl.pallas_call(close, out_shape=(jax.ShapeDtypeStruct((1, ROWS, COLS), b1...  2.83 us

profile of v6, /device:TPU:1, one launch (start us, length us, event | category | flops | bytes accessed | tf_op | source)
XLA Modules:
  0.0 54.3 jit_solution(6105427632755319055)
XLA Ops:
  0.6 50.9 %shard_map.59 = (bf16[1,640,512]{2,1,0:T(8,128)(2,1)}, f32[128,128]{1,0:T(8,128)}) custom-call(bf16[1,144,5120]{2,1,0:T(8,128)(2,1)} %act.1, bf16[1,144,512]{2,1,0:T(8,128)(2,1)} %cot.1, f32[1,640,512]{2,1,0:T(8,128)} %mom.1, f32[128,128]{1,0:T(8,128)} %constant.2.clone.table), custom_call_target="tpu_custom_call" | custom-call | flops 2000000000 | bytes 6000000 | tf_op jit(solution)/shard_map/pallas_call | solution.py:509
  51.5 2.8 %shard_map.60 = (bf16[1,640,512]{2,1,0:T(8,128)(2,1)}, f32[640,512]{1,0:T(8,128)}) custom-call(f32[128,128]{1,0:T(8,128)} %get-tuple-element.4.bands, f32[128,128]{1,0:T(8,128)} %constant.2.clone.table, bf16[1,640,512]{2,1,0:T(8,128)(2,1)} %get-tuple-element.5.value), custom_call_target="tpu_custom_call" | custom-call | flops 500000000 | bytes 4000000 | tf_op jit(solution)/shard_map/pallas_call | solution.py:551
